TPU v7x, 32 devices: a whole 2x2x4 slice. The times are simulated.
32 devices in a mesh: res: 2 (over core), dp: 16 (over z, y, x).
Axes of the slice: x: 2, y: 2, z: 4, core: 2. Of those that a mesh axis runs over, the one named last changes fastest.
Arguments:
- features: bfloat16 [2, 12544, 2048], P('res', 'dp'), may hold values from -6 to 6
- crop_counts: int32 [128], P('dp'), may hold values from 2 to 8, as said below
- crop_image: int32 [1024], P('dp'), may hold values from -1 to 127, as said below
- w_reduce: bfloat16 [2048, 512], replicated, may hold values from -0.125 to 0.125
- w_spatial: bfloat16 [4608, 512], replicated, may hold values from -0.09375 to 0.09375
- w_expand: bfloat16 [512, 2048], replicated, may hold values from -0.25 to 0.25
- w_hidden: bfloat16 [2048, 2048], replicated, may hold values from -0.125 to 0.125
- w_project: bfloat16 [2048, 128], replicated, may hold values from -0.125 to 0.125
- prototypes: bfloat16 [128, 3000], replicated, may hold values from -0.75 to 0.75
- norm_gain: float32 [5120], replicated, may hold values from 0.5 to 1.5
- norm_shift: float32 [5248], replicated, may hold values from -1.5 to 1.5
Outputs:
- loss: float32 [], replicated
- feature_grad: float32 [2, 12544, 2048], P('res', 'dp')
- reduce_grad: float32 [1048576], P(('res', 'dp'))
- spatial_grad: float32 [2359296], P(('res', 'dp'))
- expand_grad: float32 [1048576], P(('res', 'dp'))
- hidden_grad: float32 [4194304], P(('res', 'dp'))
- project_grad: float32 [262144], P(('res', 'dp'))
- prototype_grad: float32 [384000], replicated
- gain_grad: float32 [5120], replicated
- shift_grad: float32 [5248], replicated
Inputs may be any that keep to these rules, and one draw needn't show every extreme that they name: `crop_counts`: each image has 2 to 8 small crops; some image has 8 and some has 2. `crop_image`: the 64 slots of dp index d hold images d * 8 to d * 8 + 7 in any order, image i in exactly crop_counts[i] of them; the other slots hold -1.
All inputs are finite; a program needn't handle non-finite values.
Results may differ from a plain program's by a relative error of at most 0.025.
Values sent between devices are 32-bit elements; how exact they have to be, the bound alone decides.
A program may use at most 192 MiB of HBM per device.

v0:
```python
import jax
import jax.numpy as jnp
from jax import lax
from jax.sharding import PartitionSpec as P

LSIDE = 7
SSIDE = 3
SINK = 3


HIGH = lax.Precision.HIGHEST
SOFTMAX_HEAT = 0.1
SHARPNESS = 0.05
EPS_NORM = 1e-05
EPS_UNIT = 1e-06


def combined_all(part, axis, combine):
    gathered = jax.tree.map(lambda a: lax.all_gather(a, axis), part)

    def take(source):
        return jax.tree.map(lambda a: lax.dynamic_index_in_dim(a, source, 0, False), gathered)

    return lax.fori_loop(
        1, lax.axis_size(axis), lambda source, state: combine(state, take(source)), take(0)
    )


def from_behind(value, axis, steps):
    count = lax.axis_size(axis)
    leading, last = (max(0, -steps), min(count, count - steps))
    return lax.ppermute(value, axis, [(source, source + steps) for source in range(leading, last)])


def row_contract(left, right):
    return lax.dot_general(
        left, right, (((0,), (0,)), ((), ())), preferred_element_type=jnp.float32
    )


def times_transposed(left, right):
    return lax.dot_general(
        left, right, (((1,), (1,)), ((), ())), preferred_element_type=jnp.float32
    )


def split_norms(vector, width, depth):
    return (
        vector[:width],
        vector[width : 2 * width],
        vector[2 * width : 2 * width + depth],
        vector[2 * width + depth :],
    )


def displaced(values, offset):
    if offset == 0:
        return values
    filler = jnp.zeros((abs(offset),) + values.shape[1:], values.dtype)
    if offset > 0:
        return jnp.concatenate([values[offset:], filler], axis=0)
    return jnp.concatenate([filler, values[:offset]], axis=0)


def tap_layout(row_count, big_crop):
    row_ids = jnp.arange(row_count)
    side_len = jnp.where(big_crop, LSIDE, SSIDE)
    pixel = row_ids % (side_len * side_len)
    line_ids = pixel // side_len
    column_ids = pixel % side_len
    layout = []
    for tap_y in (-1, 0, 1):
        for tap_x in (-1, 0, 1):
            inside = (
                (line_ids + tap_y >= 0)
                & (line_ids + tap_y < side_len)
                & (column_ids + tap_x >= 0)
                & (column_ids + tap_x < side_len)
            )
            layout.append((inside[:, None], tap_y * LSIDE + tap_x, tap_y * SSIDE + tap_x))
    return layout


def gather_taps(acts, layout, big_crop):
    pieces = []
    for inside, step_large, step_small in layout:
        moved_rows = jnp.where(big_crop, displaced(acts, step_large), displaced(acts, step_small))
        pieces.append(jnp.where(inside, moved_rows, jnp.zeros_like(moved_rows)))
    return jnp.concatenate(pieces, axis=1)


def scatter_taps(column_grad, layout, big_crop, channels):
    result = jnp.zeros((column_grad.shape[0], channels), jnp.float32)
    for tap_index, (inside, step_large, step_small) in enumerate(layout):
        piece = column_grad[:, tap_index * channels : (tap_index + 1) * channels]
        piece = jnp.where(inside, piece, jnp.zeros_like(piece))
        result = result + jnp.where(
            big_crop, displaced(piece, -step_large), displaced(piece, -step_small)
        )
    return result


def merge_moments(first_part, second_part):
    merged_count = first_part[0] + second_part[0]
    delta = second_part[1] - first_part[1]
    merged_mean = first_part[1] + delta * (second_part[0] / merged_count)
    merged_spread = (
        first_part[2]
        + second_part[2]
        + delta * delta * (first_part[0] * second_part[0] / merged_count)
    )
    return (merged_count, merged_mean, merged_spread)


def moments(values, weight):
    row_total = jnp.sum(weight)
    local_mean = jnp.sum(values * weight, axis=0) / row_total
    centred = values - local_mean
    local_spread = jnp.sum(weight * centred * centred, axis=0)
    whole_count, mean_vec, whole_spread = combined_all(
        (row_total, local_mean, local_spread), "dp", merge_moments
    )
    return (mean_vec, whole_spread / whole_count, whole_count)


def normalize(values, weight, gain_vec, shift_vec):
    mean_vec, var_vec, whole_count = moments(values, weight)
    scale_vec = lax.rsqrt(var_vec + EPS_NORM)
    centred = (values - mean_vec) * scale_vec
    return (centred * gain_vec + shift_vec, (centred, scale_vec, whole_count))


def normalize_back(upstream, weight, gain_vec, saved_stats):
    centred, scale_vec, whole_count = saved_stats
    upstream = upstream * weight
    local_first = jnp.sum(upstream, axis=0)
    local_second = jnp.sum(upstream * centred, axis=0)
    whole_first, whole_second = lax.psum((local_first, local_second), "dp")
    result = (
        gain_vec
        * scale_vec
        * (upstream - weight * (whole_first + centred * whole_second) / whole_count)
    )
    return (result, local_second, local_first)


def gelu_back(before, upstream):
    return jax.vjp(jax.nn.gelu, before)[1](upstream)[0]


def spread_rows(crop_grad, crop_total, area):
    depth = crop_grad.shape[1]
    widened = jnp.broadcast_to(crop_grad[:crop_total, None, :], (crop_total, area, depth))
    return widened.reshape(crop_total * area, depth) / area


def body(
    features,
    crop_counts,
    crop_image,
    w_reduce,
    w_spatial,
    w_expand,
    w_hidden,
    w_project,
    prototypes,
    norm_gain,
    norm_shift,
):
    inputs = features[0]
    row_count = inputs.shape[0]
    depth = w_reduce.shape[0]
    width = w_reduce.shape[1]
    hidden = w_hidden.shape[1]
    slot_count = crop_image.shape[0]
    image_count = crop_counts.shape[0]
    image_total = image_count * lax.axis_size("dp")
    big_crop = lax.axis_index("res") == 0
    first_image = lax.axis_index("dp") * image_count
    live_slot = (crop_image >= 0).astype(jnp.float32)
    slot_rows = SSIDE * SSIDE * slot_count
    live_rows = jnp.concatenate(
        [jnp.repeat(live_slot, SSIDE * SSIDE), jnp.zeros((row_count - slot_rows,), jnp.float32)]
    )
    row_weight = jnp.where(big_crop, jnp.ones_like(live_rows), live_rows)[:, None]
    large_crops = (jnp.arange(slot_count) < 2 * image_count).astype(jnp.float32)
    crop_weight = jnp.where(big_crop, large_crops, live_slot)[:, None]
    gain_one, gain_two, gain_three, gain_four = split_norms(norm_gain, width, depth)
    shift_one, shift_two, shift_three, shift_rest = split_norms(norm_shift, width, depth)
    shift_four = shift_rest[:hidden]
    head_bias = shift_rest[hidden:]
    layout = tap_layout(row_count, big_crop)
    conv_one = jnp.dot(inputs, w_reduce, preferred_element_type=jnp.float32)
    norm_one, saved_one = normalize(conv_one, row_weight, gain_one, shift_one)
    act_one = jax.nn.gelu(norm_one).astype(jnp.bfloat16)
    columns = gather_taps(act_one, layout, big_crop)
    conv_two = jnp.dot(columns, w_spatial, preferred_element_type=jnp.float32)
    norm_two, saved_two = normalize(conv_two, row_weight, gain_two, shift_two)
    act_two = jax.nn.gelu(norm_two).astype(jnp.bfloat16)
    conv_three = jnp.dot(act_two, w_expand, preferred_element_type=jnp.float32)
    norm_three, saved_three = normalize(conv_three, row_weight, gain_three, shift_three)
    joined = norm_three + inputs.astype(jnp.float32)
    block_out = jax.nn.gelu(joined)
    large_pool = jnp.mean(block_out.reshape(2 * image_count, LSIDE * LSIDE, depth), axis=1)
    large_pool = jnp.concatenate(
        [large_pool, jnp.zeros((slot_count - 2 * image_count, depth), jnp.float32)], axis=0
    )
    small_pool = jnp.mean(block_out[:slot_rows].reshape(slot_count, SSIDE * SSIDE, depth), axis=1)
    pooled = jnp.where(big_crop, large_pool, small_pool).astype(jnp.bfloat16)
    head_one = jnp.dot(pooled, w_hidden, preferred_element_type=jnp.float32)
    norm_four, saved_four = normalize(head_one, crop_weight, gain_four, shift_four)
    act_four = jax.nn.gelu(norm_four).astype(jnp.bfloat16)
    head_two = jnp.dot(act_four, w_project, preferred_element_type=jnp.float32) + head_bias
    unit, unit_back = jax.vjp(
        lambda vec: vec * lax.rsqrt(jnp.sum(vec * vec, axis=1, keepdims=True) + EPS_UNIT), head_two
    )
    unit_low = unit.astype(jnp.bfloat16)
    scores = jnp.dot(unit_low, prototypes, preferred_element_type=jnp.float32)
    table = jnp.exp(scores[: 2 * image_count].reshape(2, image_count, -1) / SHARPNESS)
    for sweep in range(SINK):
        column_total = lax.psum(jnp.sum(table, axis=1), "dp")
        table = table / column_total[:, None, :]
        table = table / jnp.sum(table, axis=2, keepdims=True)
    own_codes = table
    far_codes = from_behind(own_codes, "res", 1)
    weight_image = 1.0 / (2.0 * (1.0 + crop_counts.astype(jnp.float32)))
    onehot = ((crop_image - first_image)[:, None] == jnp.arange(image_count)[None, :]).astype(
        jnp.float32
    )
    slot_scale = jnp.dot(onehot, weight_image, precision=HIGH) * live_slot
    small_targets = jnp.dot(onehot, far_codes[0] + far_codes[1], precision=HIGH)

    def partial_loss(scores_by_row):
        log_probability = jax.nn.log_softmax(scores_by_row / SOFTMAX_HEAT, axis=-1)
        view_zero = log_probability[:image_count]
        view_one = log_probability[image_count : 2 * image_count]
        large_share = -jnp.sum(
            weight_image
            * (
                jnp.sum(own_codes[0] * view_one, axis=-1)
                + jnp.sum(own_codes[1] * view_zero, axis=-1)
            )
        )
        small_share = -jnp.sum(slot_scale * jnp.sum(small_targets * log_probability, axis=-1))
        return jnp.where(big_crop, large_share, small_share)

    local_total, total_back = jax.vjp(partial_loss, scores)
    whole_total = lax.psum(local_total, ("res", "dp"))
    loss = whole_total / image_total
    score_grad = total_back(jnp.ones_like(local_total))[0].astype(jnp.bfloat16)
    proto_grad = row_contract(unit_low, score_grad)
    unit_grad = times_transposed(score_grad, prototypes)
    head_two_grad = unit_back(unit_grad)[0]
    bias_grad = jnp.sum(head_two_grad, axis=0)
    head_two_low = head_two_grad.astype(jnp.bfloat16)
    project_grad = row_contract(act_four, head_two_low)
    act_four_grad = times_transposed(head_two_low, w_project)
    head_one_grad, gain_four_grad, shift_four_grad = normalize_back(
        gelu_back(norm_four, act_four_grad), crop_weight, gain_four, saved_four
    )
    head_one_low = head_one_grad.astype(jnp.bfloat16)
    hidden_grad = row_contract(pooled, head_one_low)
    pooled_grad = times_transposed(head_one_low, w_hidden)
    large_spread = spread_rows(pooled_grad, 2 * image_count, LSIDE * LSIDE)
    small_spread = jnp.concatenate(
        [
            spread_rows(pooled_grad, slot_count, SSIDE * SSIDE),
            jnp.zeros((row_count - slot_rows, depth), jnp.float32),
        ],
        axis=0,
    )
    out_grad = jnp.where(big_crop, large_spread, small_spread)
    joined_grad = gelu_back(joined, out_grad)
    three_grad, gain_three_grad, shift_three_grad = normalize_back(
        joined_grad, row_weight, gain_three, saved_three
    )
    three_low = three_grad.astype(jnp.bfloat16)
    expand_grad = row_contract(act_two, three_low)
    act_two_grad = times_transposed(three_low, w_expand)
    two_grad, gain_two_grad, shift_two_grad = normalize_back(
        gelu_back(norm_two, act_two_grad), row_weight, gain_two, saved_two
    )
    two_low = two_grad.astype(jnp.bfloat16)
    spatial_grad = row_contract(columns, two_low)
    column_grad = times_transposed(two_low, w_spatial)
    act_one_grad = scatter_taps(column_grad, layout, big_crop, width)
    one_grad, gain_one_grad, shift_one_grad = normalize_back(
        gelu_back(norm_one, act_one_grad), row_weight, gain_one, saved_one
    )
    one_low = one_grad.astype(jnp.bfloat16)
    reduce_grad = row_contract(inputs, one_low)
    input_grad = (joined_grad + times_transposed(one_low, w_reduce)) * row_weight
    weight_terms = (
        reduce_grad.reshape(-1),
        spatial_grad.reshape(-1),
        expand_grad.reshape(-1),
        hidden_grad.reshape(-1),
        project_grad.reshape(-1),
    )
    summed = (
        lax.psum_scatter(weight_terms[0], ("res", "dp"), scatter_dimension=0, tiled=True),
        lax.psum_scatter(weight_terms[1], ("res", "dp"), scatter_dimension=0, tiled=True),
        lax.psum_scatter(weight_terms[2], ("res", "dp"), scatter_dimension=0, tiled=True),
        lax.psum_scatter(weight_terms[3], ("res", "dp"), scatter_dimension=0, tiled=True),
        lax.psum_scatter(weight_terms[4], ("res", "dp"), scatter_dimension=0, tiled=True),
    )
    gain_local = jnp.concatenate([gain_one_grad, gain_two_grad, gain_three_grad, gain_four_grad])
    shift_local = jnp.concatenate(
        [shift_one_grad, shift_two_grad, shift_three_grad, shift_four_grad, bias_grad]
    )
    gain_total, shift_total, proto_total = lax.psum(
        (gain_local, shift_local, proto_grad.reshape(-1)), ("res", "dp")
    )
    return (
        loss,
        input_grad[None],
        summed[0],
        summed[1],
        summed[2],
        summed[3],
        summed[4],
        proto_total,
        gain_total,
        shift_total,
    )


def solution(mesh):
    return jax.shard_map(
        body,
        mesh=mesh,
        in_specs=(P("res", "dp", None), P("dp"), P("dp"), P(), P(), P(), P(), P(), P(), P(), P()),
        out_specs=(
            P(),
            P("res", "dp", None),
            P(("res", "dp")),
            P(("res", "dp")),
            P(("res", "dp")),
            P(("res", "dp")),
            P(("res", "dp")),
            P(),
            P(),
            P(),
        ),
        check_vma=False,
    )
```

profile of v0, /device:TPU:0, one launch (start us, length us, event | category | flops | bytes accessed | tf_op | source)
XLA Modules:
  0.0 1808.8 jit_solution(6517579544279142631)
XLA Ops:
  16.0 44.0 %all-reduce.46 = (f32[16]{0:T(128)S(1)}, f32[16]{0:T(128)}) all-reduce(f32[16]{0:T(128)S(1)} %dynamic-update-slice, f32[16]{0:T(128)S(1)} %dynamic-update-slice.1), channel_id=1, replica_groups=mesh['res'=2,'dp'=16] {'dp'}, use_global_device_ids=true, to_apply=%add.33 | all-reduce | flops 32 | bytes 256
  65.2 35.6 %all-gather.8 = f32[16,1,512]{2,1,0:T(1,128)S(1)} all-gather(f32[1,1,512]{2,1,0:T(1,128)S(1)} %bitcast.221), channel_id=2, replica_groups=mesh['res'=2,'dp'=16] {'dp'}, dimensions={0}, use_global_device_ids=true | all-gather | bytes 34816 | tf_op jit(solution)/shard_map/all_gather | solution.py:19
  101.1 37.6 %all-gather.9 = f32[16,1,512]{2,1,0:T(1,128)S(1)} all-gather(f32[1,1,512]{2,1,0:T(1,128)S(1)} %bitcast.224), channel_id=3, replica_groups=mesh['res'=2,'dp'=16] {'dp'}, dimensions={0}, use_global_device_ids=true | all-gather | bytes 34816 | tf_op jit(solution)/shard_map/all_gather | solution.py:19
  138.8 39.6 %while.76 = (s32[]{:T(128)}, f32[]{:T(128)}, f32[512]{0:T(512)S(1)}, f32[512]{0:T(512)S(1)}, f32[16]{0:T(128)S(1)}, /*index=5*/f32[16,512]{1,0:T(8,128)S(1)}, f3...) while((s32[]{:T(128)}, f32[]{:T(128)}, f32[512]{0:T(512)S(1)}, f32[512]{0:T(512)S(1)}, f32[16]{0:T(128)S(1)}, ...), condition=%wide.region_4.5_spmd, body=%wide.region_3.4_spmd.sunk | while | flops 3593 | bytes 20703 | solution.py:24
  200.3 8.0 multiply_reduce_fusion.5
  209.0 35.6 %all-gather.10 = f32[16,1,512]{2,1,0:T(1,128)S(1)} all-gather(f32[1,1,512]{2,1,0:T(1,128)S(1)} %bitcast.222), channel_id=4, replica_groups=mesh['res'=2,'dp'=16] {'dp'}, dimensions={0}, use_global_device_ids=true | all-gather | bytes 34816 | tf_op jit(solution)/shard_map/all_gather | solution.py:19
  244.9 37.9 %all-gather.11 = f32[16,1,512]{2,1,0:T(1,128)S(1)} all-gather(f32[1,1,512]{2,1,0:T(1,128)S(1)} %bitcast.225), channel_id=5, replica_groups=mesh['res'=2,'dp'=16] {'dp'}, dimensions={0}, use_global_device_ids=true | all-gather | bytes 34816 | tf_op jit(solution)/shard_map/all_gather | solution.py:19
  282.8 39.6 %while.77 = (s32[]{:T(128)}, f32[]{:T(128)}, f32[512]{0:T(512)S(1)}, f32[512]{0:T(512)S(1)}, f32[16]{0:T(128)S(1)}, /*index=5*/f32[16,512]{1,0:T(8,128)S(1)}, f3...) while((s32[]{:T(128)}, f32[]{:T(128)}, f32[512]{0:T(512)S(1)}, f32[512]{0:T(512)S(1)}, f32[16]{0:T(128)S(1)}, ...), condition=%wide.region_8.9_spmd, body=%wide.region_7.8_spmd.sunk | while | flops 3593 | bytes 20703 | solution.py:24
  323.0 6.4 multiply_reduce_fusion.1
  330.1 36.2 %all-gather.4 = f32[32768]{0:T(1024)S(1)} all-gather(f32[2048]{0:T(1024)S(1)} %broadcast_divide_fusion.1), channel_id=6, replica_groups=mesh['res'=2,'dp'=16] {'dp'}, dimensions={0}, use_global_device_ids=true | all-gather | bytes 139264 | tf_op jit(solution)/shard_map/all_gather | solution.py:19
  370.0 38.1 %all-gather.5 = f32[32768]{0:T(1024)S(1)} all-gather(f32[2048]{0:T(1024)S(1)} %fusion.6), channel_id=7, replica_groups=mesh['res'=2,'dp'=16] {'dp'}, dimensions={0}, use_global_device_ids=true | all-gather | bytes 139264 | tf_op jit(solution)/shard_map/all_gather | solution.py:19
  408.2 39.7 %while.78 = (s32[]{:T(128)}, f32[]{:T(128)}, f32[2048]{0:T(1024)S(1)}, f32[2048]{0:T(1024)S(1)}, f32[16]{0:T(128)S(1)}, /*index=5*/f32[16,2048]{1,0:T(8,128)S(1)...) while((s32[]{:T(128)}, f32[]{:T(128)}, f32[2048]{0:T(1024)S(1)}, f32[2048]{0:T(1024)S(1)}, ...), condition=%wide.region_12.13_spmd, body=%wide.region_11.12_spmd.sunk | while | flops 14345 | bytes 82143 | solution.py:24
  464.7 6.3 reshape.255
  486.2 36.2 %all-gather.6 = f32[32768]{0:T(1024)S(1)} all-gather(f32[2048]{0:T(1024)S(1)} %broadcast_divide_fusion), channel_id=8, replica_groups=mesh['res'=2,'dp'=16] {'dp'}, dimensions={0}, use_global_device_ids=true | all-gather | bytes 139264 | tf_op jit(solution)/shard_map/all_gather | solution.py:19
  522.6 38.2 %all-gather.7 = f32[32768]{0:T(1024)S(1)} all-gather(f32[2048]{0:T(1024)S(1)} %fusion.40), channel_id=9, replica_groups=mesh['res'=2,'dp'=16] {'dp'}, dimensions={0}, use_global_device_ids=true | all-gather | bytes 139264 | tf_op jit(solution)/shard_map/all_gather | solution.py:19
  561.5 52.2 %while.79 = (s32[]{:T(128)}, f32[]{:T(128)}, f32[2048]{0:T(1024)S(1)}, f32[2048]{0:T(1024)S(1)}, f32[16]{0:T(128)S(1)}, /*index=5*/f32[16,2048]{1,0:T(8,128)S(1)...) while((s32[]{:T(128)}, f32[]{:T(128)}, f32[2048]{0:T(1024)S(1)}, f32[2048]{0:T(1024)S(1)}, ...), condition=%wide.region_19.20_spmd, body=%wide.region_18.19_spmd.sunk | while | flops 14345 | bytes 82143 | solution.py:24
  617.1 83.3 %psum.105 = f32[2,3000]{1,0:T(2,128)S(1)} all-reduce(f32[2,3000]{1,0:T(2,128)S(1)} %bitcast_reduce_fusion), channel_id=1, replica_groups=mesh['res'=2,'dp'=16] {'dp'}, use_global_device_ids=true, to_apply=%region_22.23 | all-reduce | flops 6000 | bytes 48000 | tf_op jit(solution)/shard_map/psum | solution.py:221
  701.3 71.7 %psum.106 = f32[2,3000]{1,0:T(2,128)S(1)} all-reduce(f32[2,3000]{1,0:T(2,128)S(1)} %fusion.52), channel_id=1, replica_groups=mesh['res'=2,'dp'=16] {'dp'}, use_global_device_ids=true, to_apply=%region_25.26 | all-reduce | flops 6000 | bytes 48000 | tf_op jit(solution)/shard_map/psum | solution.py:221
  775.2 71.7 %psum.107 = f32[2,3000]{1,0:T(2,128)S(1)} all-reduce(f32[2,3000]{1,0:T(2,128)S(1)} %fusion.54), channel_id=1, replica_groups=mesh['res'=2,'dp'=16] {'dp'}, use_global_device_ids=true, to_apply=%region_28.29 | all-reduce | flops 6000 | bytes 48000 | tf_op jit(solution)/shard_map/psum | solution.py:221
  865.6 71.7 %all-reduce.45 = (f32[2048]{0:T(1024)S(1)}, f32[2048]{0:T(1024)S(1)}) all-reduce(f32[2048]{0:T(1024)S(1)} %get-tuple-element.745, f32[2048]{0:T(1024)S(1)} %get-tuple-element.744), channel_id=1, replica_groups=mesh['res'=2,'dp'=16] {'dp'}, use_global_device_ids=true, to_apply=%region_43.44 | all-reduce | flops 4096 | bytes 32768 | tf_op jit(solution)/shard_map/psum | solution.py:138
  964.3 12.4 multiply_reduce_fusion.2
  976.7 71.7 %all-reduce.44 = (f32[2048]{0:T(1024)S(1)}, f32[2048]{0:T(1024)S(1)}) all-reduce(f32[2048]{0:T(1024)S(1)} %get-tuple-element.735, f32[2048]{0:T(1024)S(1)} %get-tuple-element.734), channel_id=1, replica_groups=mesh['res'=2,'dp'=16] {'dp'}, use_global_device_ids=true, to_apply=%region_47.48 | all-reduce | flops 4096 | bytes 32768 | tf_op jit(solution)/shard_map/psum | solution.py:138
  1058.9 37.0 %all-reduce.43 = (f32[512]{0:T(512)S(1)}, f32[512]{0:T(512)S(1)}) all-reduce(f32[512]{0:T(512)S(1)} %get-tuple-element.739, f32[512]{0:T(512)S(1)} %get-tuple-element.738), channel_id=1, replica_groups=mesh['res'=2,'dp'=16] {'dp'}, use_global_device_ids=true, to_apply=%region_51.52 | all-reduce | flops 1024 | bytes 8192 | tf_op jit(solution)/shard_map/psum | solution.py:138
  1115.0 10.9 convolution_bitcast_fusion.2
  1130.9 8.2 convolution_bitcast_fusion.1
  1146.8 8.7 fusion.86
  1155.5 38.6 %all-reduce.42 = (f32[512]{0:T(512)S(1)}, f32[512]{0:T(512)S(1)}) all-reduce(f32[512]{0:T(512)S(1)} %get-tuple-element.737, f32[512]{0:T(512)S(1)} %get-tuple-element.736), channel_id=1, replica_groups=mesh['res'=2,'dp'=16] {'dp'}, use_global_device_ids=true, to_apply=%region_55.56 | all-reduce | flops 1024 | bytes 8192 | tf_op jit(solution)/shard_map/psum | solution.py:138
  1211.5 9.7 copy.31
  1226.3 14.2 copy.33
  1247.0 40.3 %all-reduce.40 = (f32[]{:T(128)}, f32[5120]{0:T(1024)}, f32[5248]{0:T(1024)}) all-reduce(f32[]{:T(128)S(6)} %select_n.365, f32[5120]{0:T(1024)S(1)} %pad_maximum_fusion, f32[5248]{0:T(1024)S(1)} %constant_dynamic-update-slice_fusion.4), channel_id=1, replica_groups=mesh['res'=2,'dp'=16] {'res','dp'}, use_global_device_ids=true, to_apply=%region_37.38 | all-reduce | flops 10369 | bytes 82952 | tf_op jit(solution)/shard_map/psum | solution.py:248
  1287.9 8.1 multiply_bitcast_fusion
  1296.0 495.0 %all-reduce.49.cloned.1.call-done = (f32[1048576]{0:T(1024)}, f32[2359296]{0:T(1024)}, f32[1048576]{0:T(1024)}, f32[4194304]{0:T(1024)}, f32[262144]{0:T(1024)}, /*index=5*/f32[384000]{0:T(1024)}) async-done(((f32[1048576]{0:T(1024)}, f32[2359296]{0:T(1024)}, f32[1048576]{0:T(1024)}, f32[4194304]{0:T(1024)}, f32[262144]{0:T(1024)}, /*index=5*/f32[384000]{0:T(1024)}), (f32[1048576]{0:T(1024)}, ...) | async-done | bytes 37187600
  (592 shorter events, 254.9 us)
Async XLA Ops:
  7.2 315.8 %copy-start = (bf16[512,2048]{1,0:T(8,128)(2,1)S(1)}, bf16[512,2048]{1,0:T(8,128)(2,1)}, u32[]{:S(2)}) copy-start(bf16[512,2048]{1,0:T(8,128)(2,1)} %param.24) | copy-start | bytes 6291460
  7.2 1783.8 %all-reduce.49.cloned.1.call-start = ((), (), s32[]{:S(2)}) async-start(), calls=%async_computation | async-start | bytes 74375168
  8.7 439.8 %copy-start.49 = (f32[2048]{0:T(1024)}, f32[2048]{0:T(1024)S(1)}, u32[]{:S(2)}) copy-start(f32[2048]{0:T(1024)S(1)} %get-tuple-element.882) | copy-start | bytes 24580
  64.4 36.4 %copy-start.4 = (f32[784,512]{1,0:T(8,128)}, f32[784,512]{1,0:T(8,128)S(1)}, u32[]{:S(2)}) copy-start(f32[784,512]{1,0:T(8,128)S(1)} %get-tuple-element.890) | copy-start | bytes 4816900
  64.5 113.9 %copy-start.79 = (f32[5120]{0:T(1024)S(1)}, f32[5120]{0:T(1024)}, u32[]{:S(2)}) copy-start(f32[5120]{0:T(1024)} %param.28) | copy-start | bytes 61444
  64.5 113.9 %copy-start.80 = (f32[5248]{0:T(1024)S(1)}, f32[5248]{0:T(1024)}, u32[]{:S(2)}) copy-start(f32[5248]{0:T(1024)} %param.29) | copy-start | bytes 62980
  178.4 17.8 copy-start.44
  179.0 17.2 copy-start.75
  179.0 17.2 copy-start.77
  179.0 144.0 %copy-start.59 = (f32[512]{0:T(512)}, f32[512]{0:T(512)S(1)}, u32[]{:S(2)}) copy-start(f32[512]{0:T(512)S(1)} %get-tuple-element.910) | copy-start | bytes 6148
  208.3 36.3 %copy-start.7 = (f32[784,512]{1,0:T(8,128)}, f32[784,512]{1,0:T(8,128)S(1)}, u32[]{:S(2)}) copy-start(f32[784,512]{1,0:T(8,128)S(1)} %get-tuple-element.892) | copy-start | bytes 4816900
  480.4 81.0 %copy-start.128 = (f32[16]{0:T(128)S(1)}, f32[16]{0:T(128)}, u32[]{:S(2)}) copy-start(f32[16]{0:T(128)} %get-tuple-element.1219) | copy-start | bytes 196
  485.4 130.5 %copy-start.14 = (f32[64,2048]{1,0:T(8,128)}, f32[64,2048]{1,0:T(8,128)S(1)}, u32[]{:S(2)}) copy-start(f32[64,2048]{1,0:T(8,128)S(1)} %get-tuple-element.896) | copy-start | bytes 1572868
  485.4 128.9 %slice-start = ((f32[5248]{0:T(1024)}), f32[128]{0:T(128)S(1)}, s32[]{:S(2)}) async-start(f32[5248]{0:T(1024)} %param.29), calls=%async_computation.1 | async-start | bytes 1024 | tf_op jit(solution)/shard_map/slice | solution.py:191
  485.4 128.9 %copy-start.110 = (f32[2048]{0:T(1024)S(1)}, f32[2048]{0:T(1024)}, u32[]{:S(2)}) copy-start(f32[2048]{0:T(1024)} %get-tuple-element.881) | copy-start | bytes 24580
  700.5 72.8 %copy-start.120 = (f32[16]{0:T(128)}, f32[16]{0:T(128)S(1)}, u32[]{:S(2)}) copy-start(f32[16]{0:T(128)S(1)} %fusion.53) | copy-start | bytes 196
  849.4 9.2 collective-permute-start
  864.1 73.3 %copy-start.16 = (f32[64,2048]{1,0:T(8,128)S(1)}, f32[64,2048]{1,0:T(8,128)}, u32[]{:S(2)}) copy-start(f32[64,2048]{1,0:T(8,128)} %copy-done.14) | copy-start | bytes 1572868
  864.2 73.2 %copy-start.43 = (f32[2048]{0:T(1024)S(1)}, f32[2048]{0:T(1024)}, u32[]{:S(2)}) copy-start(f32[2048]{0:T(1024)} %copy-done.41) | copy-start | bytes 24580
  864.2 73.2 %copy-start.68 = (f32[2048]{0:T(1024)S(1)}, f32[2048]{0:T(1024)}, u32[]{:S(2)}) copy-start(f32[2048]{0:T(1024)} %copy-done.66) | copy-start | bytes 24580
  864.2 73.2 %copy-start.70 = (f32[2048]{0:T(1024)S(1)}, f32[2048]{0:T(1024)}, u32[]{:S(2)}) copy-start(f32[2048]{0:T(1024)} %get-tuple-element.832) | copy-start | bytes 24580
  864.2 73.2 %copy-start.103 = (f32[64]{0:T(128)S(1)}, f32[64]{0:T(128)}, u32[]{:S(2)}) copy-start(f32[64]{0:T(128)} %get-tuple-element.838) | copy-start | bytes 772
  865.6 79.0 %copy-start.71 = (f32[2048]{0:T(1024)}, f32[2048]{0:T(1024)S(1)}, u32[]{:S(2)}) copy-start(f32[2048]{0:T(1024)S(1)} %get-tuple-element.745) | copy-start | bytes 24580
  865.6 79.0 %copy-start.73 = (f32[2048]{0:T(1024)}, f32[2048]{0:T(1024)S(1)}, u32[]{:S(2)}) copy-start(f32[2048]{0:T(1024)S(1)} %get-tuple-element.744) | copy-start | bytes 24580
  964.3 84.2 %copy-start.65 = (f32[2048]{0:T(1024)S(1)}, f32[2048]{0:T(1024)}, u32[]{:S(2)}) copy-start(f32[2048]{0:T(1024)} %get-tuple-element.829) | copy-start | bytes 24580
  976.7 77.8 %copy-start.53 = (f32[2048]{0:T(1024)}, f32[2048]{0:T(1024)S(1)}, u32[]{:S(2)}) copy-start(f32[2048]{0:T(1024)S(1)} %get-tuple-element.735) | copy-start | bytes 24580
  976.7 77.8 %copy-start.55 = (f32[2048]{0:T(1024)}, f32[2048]{0:T(1024)S(1)}, u32[]{:S(2)}) copy-start(f32[2048]{0:T(1024)S(1)} %get-tuple-element.734) | copy-start | bytes 24580
  1054.6 41.3 %copy-start.105 = (f32[512]{0:T(512)S(1)}, f32[512]{0:T(512)}, u32[]{:S(2)}) copy-start(f32[512]{0:T(512)} %get-tuple-element.826) | copy-start | bytes 6148
  1058.9 37.0 %copy-start.106 = (f32[512]{0:T(512)}, f32[512]{0:T(512)S(1)}, u32[]{:S(2)}) copy-start(f32[512]{0:T(512)S(1)} %get-tuple-element.739) | copy-start | bytes 6148
  1058.9 37.0 %copy-start.108 = (f32[512]{0:T(512)}, f32[512]{0:T(512)S(1)}, u32[]{:S(2)}) copy-start(f32[512]{0:T(512)S(1)} %get-tuple-element.738) | copy-start | bytes 6148
  1146.8 47.3 %copy-start.104 = (f32[512]{0:T(512)S(1)}, f32[512]{0:T(512)}, u32[]{:S(2)}) copy-start(f32[512]{0:T(512)} %get-tuple-element.821) | copy-start | bytes 6148
  1242.9 45.1 %copy-start.34 = (bf16[2048,512]{1,0:T(8,128)(2,1)S(1)}, bf16[2048,512]{1,0:T(8,128)(2,1)}, u32[]{:S(2)}) copy-start(bf16[2048,512]{1,0:T(8,128)(2,1)} %param.22) | copy-start | bytes 6291460
  (103 other events, 421.6 us)
Sparse Core Ops, SparseCore 0:
  1243.0 547.9 all-reduce.48
where the time goes:
time: 1820 us; the launch traced here: 1810 us
  blocking collectives  825 us (45%)
  waiting for transfers between devices  495 us (27%)
  local copies, waits for them, and re-layouts  172 us (9%)
  loops' own time  121 us (7%)
  matrix products  88.7 us (5%)
  other arithmetic  84.7 us (5%)
  between operations  19.1 us (1%)
    unnamed x2, waiting for transfers between devices  495 us
    all_gather x8, blocking collectives, combined_all(): gathered = jax.tree.map(lambda a: lax.all_gather(a, axis), part)  295 us
    psum x3, blocking collectives, body(): column_total = lax.psum(jnp.sum(table, axis=1), 'dp')  227 us
    psum x4, blocking collectives, normalize_back(): whole_first, whole_second = lax.psum((local_first, local_second), 'dp')  219 us
    another operation x4, loops' own time, combined_all(): lax.fori_loop(1, lax.axis_size(axis), lambda source, state: combine(state...  121 us
    unnamed x287, local copies, waits for them, and re-layouts  59.3 us
    dynamic_slice x128, local copies, waits for them, and re-layouts, take(): lax.dynamic_index_in_dim(a, source, 0, False)  48.9 us
    unnamed x1, blocking collectives  44 us
  transfers between devices with their start and end apart: 2, of which 1 were waited for; matrix products, arithmetic and copies ran while one was open for 1% of the time, Pallas kernels for 0%

commit v1 on v0

--- a/solution.py
+++ b/solution.py
@@ -1,6 +1,8 @@
 import jax
 import jax.numpy as jnp
 from jax import lax
+from jax.experimental import pallas as pl
+from jax.experimental.pallas import tpu as pltpu
 from jax.sharding import PartitionSpec as P
 
 LSIDE = 7
@@ -325,9 +327,822 @@
     )
 
 
+MESH = pl.DeviceIdType.MESH
+BF = jnp.bfloat16
+F32 = jnp.float32
+GROUP = 16
+ROWS = 784
+WIDTH = 512
+DEPTH = 2048
+HIDDEN = 2048
+FEATS = 128
+SLOTS = 64
+IMAGES = 8
+PROTOS = 3000
+PADDED = 3072
+LANES = 128
+EDGE = 16
+STRIPE = 112
+TANH_IN = 0.7978845608
+TANH_CUBE = 0.044715
+
+X_COUNT, X_ONE, X_TWO, X_THREE, X_FOUR = 0, 1, 2, 3, 7
+X_FOUR_BACK, X_EXTRA, X_THREE_BACK, X_TWO_BACK, X_ONE_BACK, EXCHANGES = 11, 15, 16, 20, 21, 22
+
+
+def mm(left, right):
+    return jnp.dot(left, right, preferred_element_type=F32)
+
+
+def mm_t(left, right):
+    return lax.dot_general(left, right, (((1,), (1,)), ((), ())), preferred_element_type=F32)
+
+
+def t_mm(left, right):
+    return lax.dot_general(left, right, (((0,), (0,)), ((), ())), preferred_element_type=F32)
+
+
+def gelu(v):
+    return 0.5 * v * (1.0 + jnp.tanh(TANH_IN * (v + TANH_CUBE * (v * v * v))))
+
+
+def gelu_slope(v):
+    square = v * v
+    t = jnp.tanh(TANH_IN * (v + TANH_CUBE * (v * square)))
+    return 0.5 * (1.0 + t) + 0.5 * v * (1.0 - t * t) * (
+        TANH_IN * (1.0 + (3.0 * TANH_CUBE) * square)
+    )
+
+
+def two_parts(v):
+    high = v.astype(BF)
+    return high, (v - high.astype(F32)).astype(BF)
+
+
+def at(start, size):
+    return pl.ds(pl.multiple_of(start, size if size % 8 == 0 else 8), size)
+
+
+def lanes(index, width=LANES):
+    if isinstance(index, int):
+        return slice(index * width, (index + 1) * width)
+    return pl.ds(pl.multiple_of(index * width, width), width)
+
+
+def tower_kernel(
+    feat,
+    crop_row,
+    count_row,
+    w_reduce,
+    w_spatial,
+    w_expand,
+    w_hidden,
+    w_project,
+    protos,
+    gain,
+    shift,
+    loss_out,
+    feature_out,
+    reduce_out,
+    spatial_out,
+    expand_out,
+    hidden_out,
+    project_out,
+    proto_out,
+    gain_out,
+    shift_out,
+    F,
+    WR,
+    WS,
+    WE,
+    WH,
+    WP,
+    PR,
+    C1,
+    C2,
+    C3,
+    DJ,
+    DA,
+    APAD,
+    COLS,
+    A2,
+    A1T,
+    PO,
+    H1,
+    A4,
+    DA4,
+    DH1,
+    DP,
+    SC,
+    TG,
+    DS,
+    TAB,
+    Q,
+    RACC,
+    RINV,
+    UNITS,
+    UOWN,
+    RW,
+    CW,
+    LINE,
+    COL,
+    PT,
+    P,
+    PRM1,
+    PRM2,
+    PRM3,
+    PRM4,
+    MSG,
+    RECV,
+    OUTT,
+    load_sem,
+    send_sem,
+    recv_sem,
+    unit_sem,
+    out_sem,
+    far_sem,
+    FAR,
+):
+    r = lax.axis_index("res")
+    d = lax.axis_index("dp")
+    big = r == 0
+    area = jnp.where(big, LSIDE * LSIDE, SSIDE * SSIDE)
+    area_f = area.astype(F32)
+    side_f = jnp.where(big, float(LSIDE), float(SSIDE))
+    area_inv = jnp.where(big, 1.0 / (LSIDE * LSIDE), 1.0 / (SSIDE * SSIDE))
+    side_inv = jnp.where(big, 1.0 / LSIDE, 1.0 / SSIDE)
+
+    loads = [
+        pltpu.make_async_copy(source, target, load_sem.at[index])
+        for index, (source, target) in enumerate(
+            [
+                (feat.at[0], F),
+                (w_reduce, WR),
+                (w_spatial, WS),
+                (w_expand, WE),
+                (w_hidden, WH),
+                (w_project, WP),
+                (protos, PR),
+            ]
+        )
+    ]
+    for load in loads:
+        load.start()
+
+    barrier = pltpu.get_barrier_semaphore()
+
+    @pl.loop(1, GROUP)
+    def _(k):
+        pl.semaphore_signal(
+            barrier, inc=1, device_id=(r, lax.rem(d + k, GROUP)), device_id_type=MESH
+        )
+
+    pl.semaphore_signal(barrier, inc=1, device_id=(1 - r, d), device_id_type=MESH)
+
+    slot_of = lax.broadcasted_iota(jnp.int32, (ROWS, SLOTS), 1)
+    row_of = lax.broadcasted_iota(jnp.int32, (ROWS, SLOTS), 0)
+    inside = ((row_of >= slot_of * area) & (row_of < slot_of * area + area)).astype(F32)
+    lane_ids = lax.broadcasted_iota(jnp.int32, (1, SLOTS), 1)
+    crop_ids = crop_row[...]
+    live = jnp.where(big, (lane_ids < 2 * IMAGES).astype(F32), (crop_ids >= 0).astype(F32))
+    RW[...] = jnp.broadcast_to(jnp.sum(inside * live, axis=1, keepdims=True), (ROWS, LANES))
+    PT[...] = inside.astype(BF)
+    slot_row = lax.broadcasted_iota(jnp.int32, (SLOTS, ROWS), 0)
+    pixel_lane = lax.broadcasted_iota(jnp.int32, (SLOTS, ROWS), 1)
+    P[...] = (
+        ((pixel_lane >= slot_row * area) & (pixel_lane < slot_row * area + area))
+        .astype(F32)
+        .astype(BF)
+    )
+    square_row = lax.broadcasted_iota(jnp.int32, (SLOTS, SLOTS), 0)
+    square_lane = lax.broadcasted_iota(jnp.int32, (SLOTS, SLOTS), 1)
+    eye = (square_row == square_lane).astype(F32)
+    CW[...] = jnp.broadcast_to(jnp.sum(eye * live, axis=1, keepdims=True), (SLOTS, LANES))
+    live_total = jnp.sum(live, axis=1, keepdims=True)
+    own_crops = jnp.broadcast_to(live_total, (1, LANES))
+    own_rows = own_crops * area_f
+    row_f = lax.broadcasted_iota(jnp.int32, (ROWS, LANES), 0).astype(F32)
+    pixel = row_f - jnp.floor((row_f + 0.5) * area_inv) * area_f
+    line = jnp.floor((pixel + 0.5) * side_inv)
+    LINE[...] = line
+    COL[...] = pixel - line * side_f
+    APAD[0:EDGE, :] = jnp.zeros((EDGE, WIDTH), F32)
+    APAD[EDGE + ROWS :, :] = jnp.zeros((EDGE, WIDTH), F32)
+    for prm, base, blocks in ((PRM1, 0, 4), (PRM2, 4, 4), (PRM3, 8, 16), (PRM4, 24, 16)):
+        for q in range(blocks):
+            prm[q, 2:3, :] = gain[base + q : base + q + 1, :]
+            prm[q, 3:4, :] = shift[base + q : base + q + 1, :]
+    MSG[X_COUNT] = jnp.broadcast_to(own_rows, (8, LANES))
+
+    pl.semaphore_wait(barrier, GROUP)
+
+    def announce(x):
+        @pl.loop(1, GROUP)
+        def _(k):
+            pltpu.make_async_remote_copy(
+                MSG.at[x],
+                RECV.at[x, d],
+                send_sem.at[x],
+                recv_sem.at[x],
+                device_id=(r, lax.rem(d + k, GROUP)),
+                device_id_type=MESH,
+            ).start()
+
+        RECV[x, d] = MSG[x]
+
+    def collect(x):
+        others = RECV.at[x, pl.ds(0, GROUP - 1)]
+        pltpu.make_async_copy(others, others, recv_sem.at[x]).wait()
+        pltpu.make_async_copy(others, others, send_sem.at[x]).wait()
+
+    announce(X_COUNT)
+
+    def local_moments(values, rows, first_lane, weight, own, x):
+        for q in range(4):
+            v = values[rows, first_lane + q * LANES : first_lane + (q + 1) * LANES]
+            w = weight[...]
+            total = jnp.sum(v * w, axis=0, keepdims=True)
+            centred = (v - total / own) * w
+            MSG[x, q : q + 1, :] = total
+            MSG[x, 4 + q : 5 + q, :] = jnp.sum(centred * centred, axis=0, keepdims=True)
+
+    def whole_moments(x, counts, prm, first):
+        whole = jnp.sum(counts, axis=0, keepdims=True)
+        each = counts[:, None, :]
+        sums = RECV[x, :, 0:4, :]
+        spreads = RECV[x, :, 4:8, :]
+        mean = jnp.sum(sums, axis=0) / whole
+        off = sums / each - mean[None]
+        var = jnp.sum(spreads + each * off * off, axis=0) / whole
+        scale = lax.rsqrt(var + EPS_NORM)
+        for q in range(4):
+            prm[first + q, 0:1, :] = mean[q : q + 1]
+            prm[first + q, 1:2, :] = scale[q : q + 1]
+
+    def whole_back(x, whole, prm, first, place):
+        ones = jnp.sum(RECV[x, :, 0:4, :], axis=0)
+        twos = jnp.sum(RECV[x, :, 4:8, :], axis=0)
+        for q in range(4):
+            prm[first + q, 4:5, :] = ones[q : q + 1] / whole
+            prm[first + q, 5:6, :] = twos[q : q + 1] / whole
+        FAR[0, pl.ds(place, 4), :] = twos
+        FAR[0, pl.ds(48 + place, 4), :] = ones
+
+    def norm_terms(v, prm, index):
+        centred = (v - prm[index, 0:1, :]) * prm[index, 1:2, :]
+        return centred, centred * prm[index, 2:3, :] + prm[index, 3:4, :]
+
+    def back_through(du, centred, weight, prm, index):
+        inner = du - weight * (prm[index, 4:5, :] + centred * prm[index, 5:6, :])
+        return prm[index, 2:3, :] * prm[index, 1:2, :] * inner
+
+    def spread_taps(sign):
+        def for_side(side):
+            @pl.loop(0, ROWS // STRIPE)
+            def _(s):
+                base = pl.multiple_of(s * STRIPE, STRIPE)
+                rows = pl.ds(base, STRIPE)
+                window = pl.ds(base, STRIPE + 2 * EDGE)
+                for tap in range(9):
+                    dy, dx = sign * (tap // 3 - 1), sign * (tap % 3 - 1)
+                    y = LINE[rows, :] + float(dy)
+                    x = COL[rows, :] + float(dx)
+                    keep = (y >= 0.0) & (y < float(side)) & (x >= 0.0) & (x < float(side))
+                    start = EDGE + dy * side + dx
+                    for q in range(4):
+                        moved = APAD[window, lanes(q)][start : start + STRIPE]
+                        COLS[rows, tap * WIDTH + q * LANES : tap * WIDTH + (q + 1) * LANES] = (
+                            jnp.where(keep, moved, 0.0).astype(BF)
+                        )
+
+        @pl.when(big)
+        def _():
+            for_side(LSIDE)
+
+        @pl.when(jnp.logical_not(big))
+        def _():
+            for_side(SSIDE)
+
+    loads[0].wait()
+    loads[1].wait()
+    C1[...] = mm(F[...], WR[...])
+    every = pl.ds(0, ROWS)
+    local_moments(C1, every, 0, RW, own_rows, X_ONE)
+    announce(X_ONE)
+    collect(X_COUNT)
+    row_counts = RECV[X_COUNT, :, 0, :]
+    crop_counts = row_counts * area_inv
+    whole_rows = jnp.sum(row_counts, axis=0, keepdims=True)
+    whole_crops = jnp.sum(crop_counts, axis=0, keepdims=True)
+    collect(X_ONE)
+    whole_moments(X_ONE, row_counts, PRM1, 0)
+    for q in range(4):
+        _, before = norm_terms(C1[:, lanes(q)], PRM1, q)
+        act = gelu(before)
+        APAD[EDGE : EDGE + ROWS, lanes(q)] = act
+        A1T[lanes(q), :] = act.astype(BF).T
+    spread_taps(1)
+    loads[2].wait()
+
+    @pl.loop(0, 2)
+    def _(h):
+        C2[:, lanes(h, 256)] = mm(COLS[...], WS[:, lanes(h, 256)])
+
+    local_moments(C2, every, 0, RW, own_rows, X_TWO)
+    announce(X_TWO)
+    collect(X_TWO)
+    whole_moments(X_TWO, row_counts, PRM2, 0)
+    for q in range(4):
+        _, before = norm_terms(C2[:, lanes(q)], PRM2, q)
+        A2[:, lanes(q)] = gelu(before).astype(BF)
+    loads[3].wait()
+
+    @pl.loop(0, 4)
+    def _(j):
+        rows = at(j * ROWS, ROWS)
+        C3[rows, :] = mm(A2[...], WE[:, lanes(j, WIDTH)])
+        local_moments(C3, rows, 0, RW, own_rows, X_THREE + j)
+        announce(X_THREE + j)
+
+    @pl.loop(0, 4)
+    def _(j):
+        collect(X_THREE + j)
+        whole_moments(X_THREE + j, row_counts, PRM3, 4 * j)
+        rows = at(j * ROWS, ROWS)
+        for q in range(4):
+            _, before = norm_terms(C3[rows, lanes(q)], PRM3, 4 * j + q)
+            joined = before + F[:, lanes(4 * j + q)].astype(F32)
+            high, low = two_parts(gelu(joined))
+            pooled = (mm(P[...], high) + mm(P[...], low)) * area_inv
+            PO[:, lanes(4 * j + q)] = pooled.astype(BF)
+
+    loads[4].wait()
+
+    @pl.loop(0, 4)
+    def _(j):
+        H1[j] = mm(PO[...], WH[:, lanes(j, WIDTH)])
+        local_moments(H1.at[j], pl.ds(0, SLOTS), 0, CW, own_crops, X_FOUR + j)
+        announce(X_FOUR + j)
+
+    @pl.loop(0, 4)
+    def _(j):
+        collect(X_FOUR + j)
+        whole_moments(X_FOUR + j, crop_counts, PRM4, 4 * j)
+        for q in range(4):
+            _, before = norm_terms(H1[j, :, lanes(q)], PRM4, 4 * j + q)
+            A4[:, lanes(4 * j + q)] = gelu(before).astype(BF)
+
+    loads[5].wait()
+    loads[6].wait()
+    head_two = mm(A4[...], WP[...]) + shift[40:41, :]
+    length_inv = lax.rsqrt(jnp.sum(head_two * head_two, axis=1, keepdims=True) + EPS_UNIT)
+    unit = head_two * length_inv
+    unit_low = unit.astype(BF)
+    UOWN[...] = unit_low[0 : 2 * IMAGES].astype(F32)
+
+    def unit_copy(k):
+        return pltpu.make_async_remote_copy(
+            UOWN,
+            UNITS.at[d],
+            unit_sem.at[0],
+            unit_sem.at[1],
+            device_id=(r, lax.rem(d + k, GROUP)),
+            device_id_type=MESH,
+        )
+
+    forward_units = pltpu.make_async_remote_copy(
+        UNITS, UNITS, unit_sem.at[2], unit_sem.at[3], device_id=(1 - r, d), device_id_type=MESH
+    )
+
+    @pl.when(big)
+    def _():
+        @pl.loop(1, GROUP)
+        def _(k):
+            unit_copy(k).start()
+
+        UNITS[d] = UOWN[...]
+
+    SC[...] = mm(unit_low, PR[...])
+
+    @pl.when(big)
+    def _():
+        others = UNITS.at[pl.ds(0, GROUP - 1)]
+        pltpu.make_async_copy(others, others, unit_sem.at[1]).wait()
+        pltpu.make_async_copy(others, others, unit_sem.at[0]).wait()
+        forward_units.start()
+
+    @pl.when(jnp.logical_not(big))
+    def _():
+        forward_units.wait_recv()
+
+    chunk = 512
+    chunks = PADDED // chunk
+    images = GROUP * IMAGES
+    chunk_lane = lax.broadcasted_iota(jnp.int32, (1, chunk), 1)
+
+    @pl.loop(0, 2)
+    def _(v):
+        view = UNITS[:, pl.ds(pl.multiple_of(v * IMAGES, IMAGES), IMAGES), :]
+        view = view.reshape(images, FEATS).astype(BF)
+
+        def sweep(first):
+            RACC[...] = jnp.zeros_like(RACC)
+
+            @pl.loop(0, chunks)
+            def _(c):
+                columns = lanes(c, chunk)
+                valid = (chunk_lane + c * chunk) < PROTOS
+                if first:
+                    table = jnp.exp(mm(view, PR[:, columns]) / SHARPNESS)
+                else:
+                    table = TAB[:, columns] * jnp.concatenate([RINV[...]] * 4, axis=1)
+                total = jnp.sum(table, axis=0, keepdims=True)
+                table = table * jnp.where(valid, 1.0 / total, 0.0)
+                TAB[:, columns] = table
+                RACC[...] += (
+                    table[:, 0:128] + table[:, 128:256] + table[:, 256:384] + table[:, 384:512]
+                )
+
+            RINV[...] = jnp.broadcast_to(
+                1.0 / jnp.sum(RACC[...], axis=1, keepdims=True), (images, LANES)
+            )
+
+        for number in range(SINK):
+            sweep(number == 0)
+        own = pl.ds(pl.multiple_of(d * IMAGES, IMAGES), IMAGES)
+        row_inv = RINV[own, :][:, 0:1]
+        Q[pl.ds(pl.multiple_of(v * IMAGES, IMAGES), IMAGES), :] = TAB[own, :] * row_inv
+
+    ident_f = jnp.sum(eye * crop_ids.astype(F32), axis=1, keepdims=True)
+    pick_lane = lax.broadcasted_iota(jnp.int32, (SLOTS, 2 * IMAGES), 1)
+    pick_row = lax.broadcasted_iota(jnp.int32, (SLOTS, 2 * IMAGES), 0)
+    image_lane = jnp.where(pick_lane < IMAGES, pick_lane, pick_lane - IMAGES)
+    first_image = (d * IMAGES).astype(F32)
+    crossed = (pick_row < 2 * IMAGES) & (jnp.abs(pick_row - pick_lane) == IMAGES)
+    matched = ident_f == image_lane.astype(F32) + first_image
+    picked = jnp.where(big, crossed.astype(F32), matched.astype(F32))
+    image_weight = 1.0 / (2.0 * (1.0 + count_row[...].astype(F32)))
+    picked = picked * jnp.concatenate([image_weight, image_weight], axis=1)
+    TG[...] = jnp.dot(picked, Q[...], precision=HIGH, preferred_element_type=F32)
+    valid_all = lax.broadcasted_iota(jnp.int32, (1, PADDED), 1) < PROTOS
+    loss_rows = []
+    for s in range(4):
+        rows = slice(16 * s, 16 * s + 16)
+        target = TG[rows, :]
+        logit = jnp.where(valid_all, SC[rows, :] / SOFTMAX_HEAT, -1e30)
+        shifted = logit - jnp.max(logit, axis=1, keepdims=True)
+        raised = jnp.exp(shifted)
+        total = jnp.sum(raised, axis=1, keepdims=True)
+        loss_rows.append(jnp.sum(target * (shifted - jnp.log(total)), axis=1, keepdims=True))
+        mass = jnp.sum(target, axis=1, keepdims=True)
+        DS[rows, :] = ((raised * (mass / total) - target) / SOFTMAX_HEAT).astype(BF)
+    loss_local = -jnp.sum(
+        loss_rows[0] + loss_rows[1] + loss_rows[2] + loss_rows[3], axis=0, keepdims=True
+    )
+
+    OUTP = t_mm(unit_low, DS[...])
+    PROTO_BUF = TAB
+    PROTO_BUF[...] = OUTP
+    proto_copy = pltpu.make_async_copy(PROTO_BUF, proto_out, out_sem.at[2])
+    proto_copy.start()
+    unit_grad = mm_t(DS[...], PR[...])
+    along = jnp.sum(unit * unit_grad, axis=1, keepdims=True)
+    head_two_grad = (unit_grad - unit * along) * length_inv
+    bias_grad = jnp.sum(head_two_grad, axis=0, keepdims=True)
+    MSG[X_EXTRA] = jnp.concatenate(
+        [bias_grad, jnp.broadcast_to(loss_local, (1, LANES)), jnp.zeros((6, LANES), F32)], axis=0
+    )
+    announce(X_EXTRA)
+    head_two_low = head_two_grad.astype(BF)
+
+    @pl.loop(0, 4)
+    def _(j):
+        DA4[j] = mm_t(head_two_low, WP[at(j * WIDTH, WIDTH), :])
+        for q in range(4):
+            centred, before = norm_terms(H1[j, :, lanes(q)], PRM4, 4 * j + q)
+            du = DA4[j, :, lanes(q)] * gelu_slope(before) * CW[...]
+            DA4[j, :, lanes(q)] = du
+            MSG[X_FOUR_BACK + j, q : q + 1, :] = jnp.sum(du, axis=0, keepdims=True)
+            MSG[X_FOUR_BACK + j, 4 + q : 5 + q, :] = jnp.sum(du * centred, axis=0, keepdims=True)
+        announce(X_FOUR_BACK + j)
+
+    project_buf = OUTT.at[0]
+    for j in range(4):
+        project_buf[:, lanes(j)] = t_mm(A4[:, lanes(j, WIDTH)], head_two_low)
+    project_copies = [
+        pltpu.make_async_copy(
+            project_buf.at[:, lanes(j)], project_out.at[pl.ds(j * WIDTH, WIDTH), :], out_sem.at[0]
+        )
+        for j in range(4)
+    ]
+    for copy in project_copies:
+        copy.start()
+
+    @pl.loop(0, 4)
+    def _(j):
+        collect(X_FOUR_BACK + j)
+        whole_back(X_FOUR_BACK + j, whole_crops, PRM4, 4 * j, 24 + 4 * j)
+        for q in range(4):
+            centred, _ = norm_terms(H1[j, :, lanes(q)], PRM4, 4 * j + q)
+            DH1[:, lanes(4 * j + q)] = back_through(
+                DA4[j, :, lanes(q)], centred, CW[...], PRM4, 4 * j + q
+            ).astype(BF)
+
+    @pl.loop(0, 4)
+    def _(j):
+        DP[j] = mm_t(DH1[...], WH[at(j * WIDTH, WIDTH), :]) * area_inv
+
+    @pl.loop(0, 4)
+    def _(j):
+        rows = at(j * ROWS, ROWS)
+        for q in range(4):
+            high, low = two_parts(DP[j, :, lanes(q)])
+            out_grad = mm(PT[...], high) + mm(PT[...], low)
+            centred, before = norm_terms(C3[rows, lanes(q)], PRM3, 4 * j + q)
+            joined = before + F[:, lanes(4 * j + q)].astype(F32)
+            du = out_grad * gelu_slope(joined)
+            DJ[rows, lanes(q)] = du
+            MSG[X_THREE_BACK + j, q : q + 1, :] = jnp.sum(du, axis=0, keepdims=True)
+            MSG[X_THREE_BACK + j, 4 + q : 5 + q, :] = jnp.sum(du * centred, axis=0, keepdims=True)
+        announce(X_THREE_BACK + j)
+
+    pltpu.make_async_copy(project_buf, project_buf, out_sem.at[0]).wait()
+
+    def send_tile(slot, target, first):
+        copy = pltpu.make_async_copy(OUTT.at[slot], target, out_sem.at[slot])
+        if not isinstance(first, bool):
+
+            @pl.when(jnp.logical_not(first))
+            def _():
+                copy.wait()
+        elif not first:
+            copy.wait()
+        return copy
+
+    @pl.loop(0, 16)
+    def _(tile):
+        slot = lax.rem(tile, 2)
+        i = tile // 4
+        j = lax.rem(tile, 4)
+        target = hidden_out.at[at(i * WIDTH, WIDTH), lanes(j, WIDTH)]
+        copy = send_tile(slot, target, tile < 2)
+        OUTT[slot] = t_mm(PO[:, lanes(i, WIDTH)], DH1[:, lanes(j, WIDTH)])
+        copy.start()
+
+    @pl.loop(0, 4)
+    def _(j):
+        collect(X_THREE_BACK + j)
+        whole_back(X_THREE_BACK + j, whole_rows, PRM3, 4 * j, 8 + 4 * j)
+        rows = at(j * ROWS, ROWS)
+        for q in range(4):
+            centred, _ = norm_terms(C3[rows, lanes(q)], PRM3, 4 * j + q)
+            COLS[:, lanes(4 * j + q)] = back_through(
+                DJ[rows, lanes(q)], centred, RW[...], PRM3, 4 * j + q
+            ).astype(BF)
+
+    @pl.loop(0, 2)
+    def _(h):
+        DA[:, lanes(h, 256)] = mm_t(COLS[:, 0:DEPTH], WE[at(h * 256, 256), :])
+
+    for q in range(4):
+        centred, before = norm_terms(C2[:, lanes(q)], PRM2, q)
+        du = DA[:, lanes(q)] * gelu_slope(before) * RW[...]
+        DA[:, lanes(q)] = du
+        MSG[X_TWO_BACK, q : q + 1, :] = jnp.sum(du, axis=0, keepdims=True)
+        MSG[X_TWO_BACK, 4 + q : 5 + q, :] = jnp.sum(du * centred, axis=0, keepdims=True)
+    announce(X_TWO_BACK)
+
+    @pl.loop(0, 4)
+    def _(j):
+        slot = lax.rem(j, 2)
+        copy = send_tile(slot, expand_out.at[:, lanes(j, WIDTH)], False)
+        OUTT[slot] = t_mm(A2[...], COLS[:, lanes(j, WIDTH)])
+        copy.start()
+
+    collect(X_TWO_BACK)
+    whole_back(X_TWO_BACK, whole_rows, PRM2, 0, 4)
+    for q in range(4):
+        centred, _ = norm_terms(C2[:, lanes(q)], PRM2, q)
+        APAD[EDGE : EDGE + ROWS, lanes(q)] = back_through(
+            DA[:, lanes(q)], centred, RW[...], PRM2, q
+        )
+    spread_taps(-1)
+
+    @pl.loop(0, 2)
+    def _(h):
+        total = mm_t(COLS[:, 0:WIDTH], WS[at(h * 256, 256), :])
+        for tap in range(1, 9):
+            total += mm_t(
+                COLS[:, tap * WIDTH : (tap + 1) * WIDTH], WS[at(tap * WIDTH + h * 256, 256), :]
+            )
+        DA[:, lanes(h, 256)] = total
+
+    for q in range(4):
+        centred, before = norm_terms(C1[:, lanes(q)], PRM1, q)
+        du = DA[:, lanes(q)] * gelu_slope(before) * RW[...]
+        DA[:, lanes(q)] = du
+        MSG[X_ONE_BACK, q : q + 1, :] = jnp.sum(du, axis=0, keepdims=True)
+        MSG[X_ONE_BACK, 4 + q : 5 + q, :] = jnp.sum(du * centred, axis=0, keepdims=True)
+    announce(X_ONE_BACK)
+
+    @pl.loop(0, 9)
+    def _(tap):
+        slot = lax.rem(tap, 2)
+        copy = send_tile(slot, spatial_out.at[at(tap * WIDTH, WIDTH), :], False)
+        OUTT[slot] = mm(A1T[...], COLS[:, lanes(tap, WIDTH)])
+        copy.start()
+
+    collect(X_ONE_BACK)
+    whole_back(X_ONE_BACK, whole_rows, PRM1, 0, 0)
+    collect(X_EXTRA)
+    extra = jnp.sum(RECV[X_EXTRA], axis=0)
+    FAR[0, 88:96, :] = extra
+    far = pltpu.make_async_remote_copy(
+        FAR.at[0],
+        FAR.at[1],
+        far_sem.at[0],
+        far_sem.at[1],
+        device_id=(1 - r, d),
+        device_id_type=MESH,
+    )
+    far.start()
+    for q in range(4):
+        centred, _ = norm_terms(C1[:, lanes(q)], PRM1, q)
+        A2[:, lanes(q)] = back_through(DA[:, lanes(q)], centred, RW[...], PRM1, q).astype(BF)
+
+    @pl.loop(0, 4)
+    def _(j):
+        rows = at(j * ROWS, ROWS)
+        grad = mm_t(A2[...], WR[at(j * WIDTH, WIDTH), :])
+        for q in range(4):
+            DJ[rows, lanes(q)] = (DJ[rows, lanes(q)] + grad[:, lanes(q)]) * RW[...]
+        pltpu.make_async_copy(
+            DJ.at[rows, :], feature_out.at[0, :, lanes(j, WIDTH)], out_sem.at[3]
+        ).start()
+
+    @pl.loop(0, 4)
+    def _(j):
+        slot = lax.rem(j + 1, 2)
+        copy = send_tile(slot, reduce_out.at[at(j * WIDTH, WIDTH), :], False)
+        OUTT[slot] = t_mm(F[:, lanes(j, WIDTH)], A2[...])
+        copy.start()
+
+    far.wait()
+    both = jnp.where(big, FAR[0], FAR[1]) + jnp.where(big, FAR[1], FAR[0])
+    gain_out[...] = both[0:40]
+    shift_out[0:40, :] = both[48:88]
+    shift_out[40:41, :] = both[88:89]
+    loss_out[...] = jnp.broadcast_to(both[89:90], (8, LANES)) / float(GROUP * IMAGES)
+
+    @pl.when(big)
+    def _():
+        forward_units.wait_send()
+
+    proto_copy.wait()
+    for slot in range(2):
+        pltpu.make_async_copy(
+            OUTT.at[slot], reduce_out.at[pl.ds(0, WIDTH), :], out_sem.at[slot]
+        ).wait()
+    pltpu.make_async_copy(feature_out.at[0], feature_out.at[0], out_sem.at[3]).wait()
+
+
+def tower(
+    features,
+    crop_counts,
+    crop_image,
+    w_reduce,
+    w_spatial,
+    w_expand,
+    w_hidden,
+    w_project,
+    prototypes,
+    norm_gain,
+    norm_shift,
+):
+    protos = jnp.pad(prototypes, ((0, 0), (0, PADDED - PROTOS)))
+    anywhere = pl.BlockSpec(memory_space=pl.ANY)
+    inside = pl.BlockSpec(memory_space=pltpu.VMEM)
+
+    def vm(*shape, dtype=F32):
+        return pltpu.VMEM(shape, dtype)
+
+    dma = pltpu.SemaphoreType.DMA
+
+    def shaped(*shape):
+        return jax.ShapeDtypeStruct(shape, F32)
+
+    return pl.pallas_call(
+        tower_kernel,
+        out_shape=(
+            shaped(8, LANES),
+            shaped(1, ROWS, DEPTH),
+            shaped(DEPTH, WIDTH),
+            shaped(9 * WIDTH, WIDTH),
+            shaped(WIDTH, DEPTH),
+            shaped(DEPTH, HIDDEN),
+            shaped(HIDDEN, FEATS),
+            shaped(FEATS, PADDED),
+            shaped(40, LANES),
+            shaped(41, LANES),
+        ),
+        in_specs=[anywhere, inside, inside] + [anywhere] * 6 + [inside, inside],
+        out_specs=(inside,) + (anywhere,) * 7 + (inside, inside),
+        scratch_shapes=[
+            vm(ROWS, DEPTH, dtype=BF),
+            vm(DEPTH, WIDTH, dtype=BF),
+            vm(9 * WIDTH, WIDTH, dtype=BF),
+            vm(WIDTH, DEPTH, dtype=BF),
+            vm(DEPTH, HIDDEN, dtype=BF),
+            vm(HIDDEN, FEATS, dtype=BF),
+            vm(FEATS, PADDED, dtype=BF),
+            vm(ROWS, WIDTH),
+            vm(ROWS, WIDTH),
+            vm(4 * ROWS, WIDTH),
+            vm(4 * ROWS, WIDTH),
+            vm(ROWS, WIDTH),
+            vm(ROWS + 2 * EDGE, WIDTH),
+            vm(ROWS, 9 * WIDTH, dtype=BF),
+            vm(ROWS, WIDTH, dtype=BF),
+            vm(WIDTH, ROWS, dtype=BF),
+            vm(SLOTS, DEPTH, dtype=BF),
+            vm(4, SLOTS, WIDTH),
+            vm(SLOTS, HIDDEN, dtype=BF),
+            vm(4, SLOTS, WIDTH),
+            vm(SLOTS, HIDDEN, dtype=BF),
+            vm(4, SLOTS, WIDTH),
+            vm(SLOTS, PADDED),
+            vm(SLOTS, PADDED),
+            vm(SLOTS, PADDED, dtype=BF),
+            vm(GROUP * IMAGES, PADDED),
+            vm(2 * IMAGES, PADDED),
+            vm(GROUP * IMAGES, LANES),
+            vm(GROUP * IMAGES, LANES),
+            vm(GROUP, 2 * IMAGES, FEATS),
+            vm(2 * IMAGES, FEATS),
+            vm(ROWS, LANES),
+            vm(SLOTS, LANES),
+            vm(ROWS, LANES),
+            vm(ROWS, LANES),
+            vm(ROWS, SLOTS, dtype=BF),
+            vm(SLOTS, ROWS, dtype=BF),
+            vm(4, 8, LANES),
+            vm(4, 8, LANES),
+            vm(16, 8, LANES),
+            vm(16, 8, LANES),
+            vm(EXCHANGES, 8, LANES),
+            vm(EXCHANGES, GROUP, 8, LANES),
+            vm(2, WIDTH, WIDTH),
+            dma((7,)),
+            dma((EXCHANGES,)),
+            dma((EXCHANGES,)),
+            dma((4,)),
+            dma((4,)),
+            dma((2,)),
+            vm(2, 96, LANES),
+        ],
+        compiler_params=pltpu.CompilerParams(
+            collective_id=0, has_side_effects=True, vmem_limit_bytes=62 << 20
+        ),
+    )(
+        features,
+        crop_image.reshape(1, SLOTS),
+        crop_counts.reshape(1, IMAGES),
+        w_reduce,
+        w_spatial,
+        w_expand,
+        w_hidden,
+        w_project,
+        protos,
+        norm_gain.reshape(40, LANES),
+        norm_shift.reshape(41, LANES),
+    )
+
+
+def fused_body(*arrays):
+    loss, feature_grad, reduce, spatial, expand, hidden, project, proto, gain, shift = tower(*arrays)
+
+    def scattered(grad):
+        return lax.psum_scatter(
+            grad.reshape(-1), ("res", "dp"), scatter_dimension=0, tiled=True
+        )
+
+    return (
+        loss[0, 0],
+        feature_grad,
+        scattered(reduce),
+        scattered(spatial),
+        scattered(expand),
+        scattered(hidden),
+        scattered(project),
+        lax.psum(proto[:, :PROTOS].reshape(-1), ("res", "dp")),
+        gain.reshape(-1),
+        shift.reshape(-1),
+    )
+
+
 def solution(mesh):
     return jax.shard_map(
-        body,
+        fused_body if mesh.shape["dp"] == GROUP else body,
         mesh=mesh,
         in_specs=(P("res", "dp", None), P("dp"), P("dp"), P(), P(), P(), P(), P(), P(), P(), P()),
         out_specs=(

time: 1820 us -> 747 us (0.41)
  blocking collectives: 825 us -> 0 us
  Pallas kernels: 0 us -> 127 us
  loops' own time: 121 us -> 0 us
  local copies, waits for them, and re-layouts: 172 us -> 57 us
  matrix products: 88.7 us -> 0 us
  other arithmetic: 84.7 us -> 0 us
  waiting for transfers between devices: 495 us -> 549 us
    psum x8 -> x0, blocking collectives: 486 us -> none  [the longest x3 227 us: body(): column_total = lax.psum(jnp.sum(table, axis=1), 'dp')]
    all_gather x8 -> x0, blocking collectives: 295 us -> none  [combined_all(): gathered = jax.tree.map(lambda a: lax.all_gather(a, axis), part)]
    pallas_call x0 -> x1, Pallas kernels: none -> 127 us  [tower(): pl.pallas_call(tower_kernel, out_shape=(shaped(8, LANES), shaped(1, ROWS,...]
    another operation x4 -> x0, loops' own time: 121 us -> none  [combined_all(): lax.fori_loop(1, lax.axis_size(axis), lambda source, state: combine(state...]
    dot_general x20 -> x0, matrix products: 88.7 us -> none  [the longest x6 31.5 us: row_contract(): lax.dot_general(left, right, (((0,), (0,)), ((), ())), preferred_element_...]
    unnamed x2, waiting for transfers between devices: 495 us -> 549 us
    dynamic_slice x128 -> x0, local copies, waits for them, and re-layouts: 48.9 us -> none  [take(): lax.dynamic_index_in_dim(a, source, 0, False)]
    unnamed x1 -> x0, blocking collectives: 44 us -> none
  transfers between devices with their start and end apart: 2 -> 1, of which waited for: 1 -> 1; matrix products, arithmetic and copies ran while one was open for 1% -> 0% of each run, Pallas kernels for 0% -> 0%
where the time goes in v1:
time: 747 us
  waiting for transfers between devices  549 us (73%)
  Pallas kernels  127 us (17%)
  local copies, waits for them, and re-layouts  57 us (8%)
  between operations  14.1 us (2%)
    unnamed x2, waiting for transfers between devices  549 us
    pallas_call x1, Pallas kernels, tower(): pl.pallas_call(tower_kernel, out_shape=(shaped(8, LANES), shaped(1, ROWS,...  127 us
    unnamed x22, local copies, waits for them, and re-layouts  52.7 us
  transfers between devices with their start and end apart: 1, of which 1 were waited for; matrix products, arithmetic and copies ran while one was open for 0% of the time, Pallas kernels for 0%

profile of v1, /device:TPU:0, one launch (start us, length us, event | category | flops | bytes accessed | tf_op | source)
XLA Modules:
  0.0 746.9 jit_solution(2475338280064201249)
XLA Ops:
  7.2 0.0 all-reduce.9.cloned.1.call-start
  7.2 1.4 copy.23
  8.7 0.9 pad.4.protos
  9.6 126.6 %shard_map.186 = (f32[8,128]{1,0:T(8,128)}, f32[1,784,2048]{2,1,0:T(8,128)}, f32[2048,512]{1,0:T(8,128)}, f32[4608,512]{1,0:T(8,128)}, f32[512,2048]{1,0:T(8,128...) custom-call(bf16[1,784,2048]{2,1,0:T(8,128)(2,1)} %feat.1, ...), custom_call_target="tpu_custom_call" | custom-call | tf_op jit(solution)/shard_map/pallas_call | solution.py:1034
  136.2 5.3 copy.24
  141.5 9.7 %copy.25 = f32[576,4,8,128]{3,1,2,0:T(4,128)} copy(f32[576,4,8,128]{3,2,1,0:T(8,128)} %bitcast.22) | data formatting | bytes 18874368
  151.2 5.0 copy.26
  156.2 0.0 copy-start
  156.2 14.2 %copy.27 = f32[256,16,8,128]{3,1,2,0:T(8,128)} copy(f32[256,16,8,128]{3,2,1,0:T(8,128)} %bitcast.21) | data formatting | bytes 33554432
  170.4 0.0 copy-done
  170.4 2.2 reshape.65
  172.7 0.0 all-reduce.9.cloned.1.call-update
  172.7 1.2 slice.6
  173.9 549.1 %all-reduce.9.cloned.1.call-done = (f32[1048576]{0:T(1024)}, f32[2359296]{0:T(1024)}, f32[1048576]{0:T(1024)}, f32[4194304]{0:T(1024)}, f32[262144]{0:T(1024)}, /*index=5*/f32[384000]{0:T(1024)}) async-done(((f32[1048576]{0:T(1024)}, f32[2359296]{0:T(1024)}, f32[1048576]{0:T(1024)}, f32[4194304]{0:T(1024)}, f32[262144]{0:T(1024)}, /*index=5*/f32[384000]{0:T(1024)}), (f32[1048576]{0:T(1024)}, ...) | async-done | bytes 37187600
  723.0 1.6 dynamic-slice
  724.5 1.6 dynamic-slice.2
  726.1 1.7 dynamic-slice.1
  727.8 1.9 dynamic-slice.3
  729.7 1.4 dynamic-slice.4
  731.1 0.0 copy-start.1
  731.1 0.0 copy-start.3
  731.1 0.0 copy-start.2
  731.1 6.5 copy.37
  737.6 0.0 copy-done.1
  737.6 1.2 copy.38
  738.8 0.0 copy-done.3
  738.8 0.6 copy.39
  739.4 0.0 copy-done.2
  739.4 0.6 copy.40
Async XLA Ops:
  7.2 715.8 %all-reduce.9.cloned.1.call-start = ((), (), s32[]{:S(2)}) async-start(), calls=%async_computation | async-start | bytes 74375168
  156.2 14.2 %copy-start = (f32[128,3072]{1,0:T(8,128)S(1)}, f32[128,3072]{1,0:T(8,128)}, u32[]{:S(2)}) copy-start(f32[128,3072]{1,0:T(8,128)} %get-tuple-element.27) | copy-start | bytes 4718596
  731.1 6.5 copy-start.1
  731.1 7.7 %copy-start.3 = (f32[40,128]{1,0:T(8,128)S(1)}, f32[40,128]{1,0:T(8,128)}, u32[]{:S(2)}) copy-start(f32[40,128]{1,0:T(8,128)} %get-tuple-element.28) | copy-start | bytes 61444
  731.1 8.3 %copy-start.2 = (f32[41,128]{1,0:T(8,128)S(1)}, f32[41,128]{1,0:T(8,128)}, u32[]{:S(2)}) copy-start(f32[41,128]{1,0:T(8,128)} %get-tuple-element.29) | copy-start | bytes 62980
Sparse Core Ops, SparseCore 0:
  172.8 550.1 all-reduce.8

commit v2 on v1

--- a/solution.py
+++ b/solution.py
@@ -348,6 +348,8 @@
 
 X_COUNT, X_ONE, X_TWO, X_THREE, X_FOUR = 0, 1, 2, 3, 7
 X_FOUR_BACK, X_EXTRA, X_THREE_BACK, X_TWO_BACK, X_ONE_BACK, EXCHANGES = 11, 15, 16, 20, 21, 22
+SPATIAL_HALF = 2304
+PROTO_HALF = 1536
 
 
 def mm(left, right):
@@ -411,18 +413,23 @@
     proto_out,
     gain_out,
     shift_out,
+    PG,
+    RB_S,
+    RB_R,
+    RB_E,
+    RB_P,
     F,
     WR,
     WS,
     WE,
-    WH,
+    WHB,
+    WHC,
     WP,
     PR,
     C1,
     C2,
     C3,
     DJ,
-    DA,
     APAD,
     COLS,
     A2,
@@ -432,10 +439,11 @@
     A4,
     DA4,
     DH1,
-    DP,
-    SC,
-    TG,
     DS,
+    UL,
+    POF,
+    D2F,
+    D2A,
     TAB,
     Q,
     RACC,
@@ -454,14 +462,35 @@
     PRM4,
     MSG,
     RECV,
-    OUTT,
+    FAR,
+    OUT,
+    RC_E,
+    RC_P,
+    OUT_P,
+    STG,
+    STGE,
+    HACC,
+    HREC,
+    HAL,
+    PACC,
+    PREC,
+    PIN,
     load_sem,
     send_sem,
     recv_sem,
     unit_sem,
     out_sem,
     far_sem,
-    FAR,
+    wh_sem,
+    rs_send,
+    rs_recv,
+    stage_sem,
+    gather_send,
+    gather_recv,
+    core_send,
+    core_recv,
+    row_sem,
+    free_sem,
 ):
     r = lax.axis_index("res")
     d = lax.axis_index("dp")
@@ -480,7 +509,7 @@
                 (w_reduce, WR),
                 (w_spatial, WS),
                 (w_expand, WE),
-                (w_hidden, WH),
+                (w_hidden.at[:, pl.ds(pl.multiple_of(d * LANES, LANES), LANES)], WHC),
                 (w_project, WP),
                 (protos, PR),
             ]
@@ -488,6 +517,14 @@
     ]
     for load in loads:
         load.start()
+
+    def hidden_load(k, slot):
+        return pltpu.make_async_copy(
+            w_hidden.at[:, lanes(k, 256)], WHB.at[slot], wh_sem.at[slot]
+        )
+
+    for k in range(2):
+        hidden_load(k, k).start()
 
     barrier = pltpu.get_barrier_semaphore()
 
@@ -556,6 +593,163 @@
         pltpu.make_async_copy(others, others, send_sem.at[x]).wait()
 
     announce(X_COUNT)
+
+    place = {1: lax.rem(d, 2), 2: lax.rem(d // 2, 2), 4: lax.rem(d // 4, 2), 8: d // 8}
+
+    def partner(bit):
+        return (r, d + bit * (1 - 2 * place[bit]))
+
+    def block_of(order, stage, j, flip):
+        index = 0
+        for t, bit in enumerate(order):
+            if t < stage:
+                index = index + bit * place[bit]
+            elif t == stage:
+                index = index + bit * ((1 - place[bit]) if flip else place[bit])
+            else:
+                index = index + bit * ((j >> (t - stage - 1)) & 1)
+        return index
+
+    class Strip:
+        def __init__(self, own, base, depth, columns, landing, staging, order, number):
+            self.own, self.base, self.depth, self.columns = own, base, depth, columns
+            self.landing, self.staging, self.order, self.number = landing, staging, order, number
+
+        def block(self, index):
+            start = pl.multiple_of(self.base + index * self.depth, 16)
+            return self.own.at[pl.ds(start, self.depth), self.columns]
+
+        def rows(self, stage):
+            first = 16 - (16 >> stage)
+            return first * self.depth, (8 >> stage) * self.depth
+
+        def start(self, stage):
+            first, _ = self.rows(stage)
+            for j in range(8 >> stage):
+                pltpu.make_async_remote_copy(
+                    self.block(block_of(self.order, stage, j, True)),
+                    self.landing.at[pl.ds(first + j * self.depth, self.depth), :],
+                    rs_send.at[self.number, stage],
+                    rs_recv.at[self.number, stage],
+                    device_id=partner(self.order[stage]),
+                    device_id_type=MESH,
+                ).start()
+
+        def landed(self, stage):
+            first, size = self.rows(stage)
+            return self.landing.at[pl.ds(first, size), :]
+
+        def fetch(self, stage, slot):
+            area = self.landed(stage)
+            pltpu.make_async_copy(area, area, rs_recv.at[self.number, stage]).wait()
+            _, size = self.rows(stage)
+            copy = pltpu.make_async_copy(
+                area, self.staging.at[slot, pl.ds(0, size), :], stage_sem.at[slot]
+            )
+            copy.start()
+            return copy
+
+        def fold(self, stage, slot):
+            for j in range(8 >> stage):
+                target = self.block(block_of(self.order, stage, j, False))
+                target[...] += self.staging[slot, j * self.depth : (j + 1) * self.depth, :]
+
+        def close(self):
+            for stage in range(4):
+                area = self.landed(stage)
+                pltpu.make_async_copy(area, area, rs_send.at[self.number, stage]).wait()
+
+    def advance(steps):
+        copies = [steps[0][0].fetch(steps[0][1], 0)]
+        for k, (strip, stage) in enumerate(steps):
+            if k + 1 < len(steps):
+                copies.append(steps[k + 1][0].fetch(steps[k + 1][1], (k + 1) % 2))
+            copies[k].wait()
+            strip.fold(stage, k % 2)
+            if stage < 3:
+                strip.start(stage + 1)
+
+    order_a, order_b, order_c = (1, 2, 4, 8), (2, 1, 4, 8), (4, 1, 2, 8)
+    orders = (order_a, order_b, order_b, order_c)
+    spatial_strips = [
+        Strip(C3, 0, 144, lanes(q), RB_S.at[q], STG, orders[q], q) for q in range(4)
+    ]
+    reduce_strips = [
+        Strip(C3, SPATIAL_HALF, 64, lanes(q), RB_R.at[q], STG, orders[q], 4 + q) for q in range(4)
+    ]
+    expand_strips = [
+        Strip(RC_E, 256 * q, 16, slice(0, WIDTH), RB_E.at[q], STGE, orders[q], 8 + q)
+        for q in range(4)
+    ]
+    proto_strip = Strip(RC_P, 0, 96, slice(0, LANES), RB_P, STG, order_c, 12)
+
+    def gathered_block(order, stage, j):
+        index = 0
+        for t, bit in enumerate(order):
+            if t < stage:
+                index = index + bit * ((j >> t) & 1)
+            else:
+                index = index + bit * place[bit]
+        return index
+
+    def gather_start(ref, base, depth, columns, order, stage, number):
+        for j in range(1 << stage):
+            start = pl.multiple_of(base + gathered_block(order, stage, j) * depth, 16)
+            area = ref.at[pl.ds(start, depth), columns]
+            pltpu.make_async_remote_copy(
+                area,
+                area,
+                gather_send.at[number, stage],
+                gather_recv.at[number, stage],
+                device_id=partner(order[stage]),
+                device_id_type=MESH,
+            ).start()
+
+    def gather_wait(ref, depth, columns, stage, number, sems):
+        area = ref.at[pl.ds(0, depth << stage), columns]
+        pltpu.make_async_copy(area, area, sems.at[number, stage]).wait()
+
+    pooled_parts = (
+        (slice(0, 640), (8, 4, 2, 1)),
+        (slice(640, 1536), (8, 4, 1, 2)),
+        (slice(1536, 2048), (8, 2, 1, 4)),
+    )
+
+    def by_size(action):
+        @pl.when(big)
+        def _():
+            action(2 * IMAGES)
+
+        @pl.when(jnp.logical_not(big))
+        def _():
+            action(SLOTS)
+
+    def pooled_gather(stage):
+        def action(depth):
+            for number, (columns, order) in enumerate(pooled_parts):
+                gather_start(PG, 0, depth, columns, order, stage, number)
+
+        by_size(action)
+
+    def pooled_arrived(stage):
+        def action(depth):
+            for number, (columns, order) in enumerate(pooled_parts):
+                gather_wait(PG, depth, columns, stage, number, gather_recv)
+
+        by_size(action)
+
+    def core_copy(source, target, sent, landed):
+        return pltpu.make_async_remote_copy(
+            source,
+            target,
+            core_send.at[sent],
+            core_recv.at[landed],
+            device_id=(1 - r, d),
+            device_id_type=MESH,
+        )
+
+    def half_tile(index):
+        return pl.ds(pl.multiple_of(index * 256, 256), 256)
 
     def local_moments(values, rows, first_lane, weight, own, x):
         for q in range(4):
@@ -674,13 +868,29 @@
             joined = before + F[:, lanes(4 * j + q)].astype(F32)
             high, low = two_parts(gelu(joined))
             pooled = (mm(P[...], high) + mm(P[...], low)) * area_inv
-            PO[:, lanes(4 * j + q)] = pooled.astype(BF)
-
-    loads[4].wait()
+            pooled_low = pooled.astype(BF)
+            PO[:, lanes(4 * j + q)] = pooled_low
+            POF[:, lanes(4 * j + q)] = pooled_low.astype(F32) * CW[...]
+
+    def keep_pooled(depth):
+        copy = pltpu.make_async_copy(
+            POF.at[pl.ds(0, depth), :],
+            PG.at[pl.ds(pl.multiple_of(d * depth, 16), depth), :],
+            row_sem.at[0],
+        )
+        copy.start()
+        copy.wait()
+
+    by_size(keep_pooled)
+    pooled_gather(0)
 
     @pl.loop(0, 4)
     def _(j):
-        H1[j] = mm(PO[...], WH[:, lanes(j, WIDTH)])
+        for half in range(2):
+            k = 2 * j + half
+            hidden_load(k, half).wait()
+            H1[j, :, half * 256 : half * 256 + 256] = mm(PO[...], WHB[half])
+            hidden_load(lax.rem(k + 2, 8), half).start()
         local_moments(H1.at[j], pl.ds(0, SLOTS), 0, CW, own_crops, X_FOUR + j)
         announce(X_FOUR + j)
 
@@ -692,6 +902,8 @@
             _, before = norm_terms(H1[j, :, lanes(q)], PRM4, 4 * j + q)
             A4[:, lanes(4 * j + q)] = gelu(before).astype(BF)
 
+    pooled_arrived(0)
+    pooled_gather(1)
     loads[5].wait()
     loads[6].wait()
     head_two = mm(A4[...], WP[...]) + shift[40:41, :]
@@ -699,6 +911,7 @@
     unit = head_two * length_inv
     unit_low = unit.astype(BF)
     UOWN[...] = unit_low[0 : 2 * IMAGES].astype(F32)
+    UL[...] = unit_low
 
     def unit_copy(k):
         return pltpu.make_async_remote_copy(
@@ -722,8 +935,6 @@
 
         UNITS[d] = UOWN[...]
 
-    SC[...] = mm(unit_low, PR[...])
-
     @pl.when(big)
     def _():
         others = UNITS.at[pl.ds(0, GROUP - 1)]
@@ -735,6 +946,9 @@
     def _():
         forward_units.wait_recv()
 
+    pooled_arrived(1)
+    pooled_gather(2)
+
     chunk = 512
     chunks = PADDED // chunk
     images = GROUP * IMAGES
@@ -753,15 +967,17 @@
                 columns = lanes(c, chunk)
                 valid = (chunk_lane + c * chunk) < PROTOS
                 if first:
-                    table = jnp.exp(mm(view, PR[:, columns]) / SHARPNESS)
-                else:
-                    table = TAB[:, columns] * jnp.concatenate([RINV[...]] * 4, axis=1)
-                total = jnp.sum(table, axis=0, keepdims=True)
-                table = table * jnp.where(valid, 1.0 / total, 0.0)
-                TAB[:, columns] = table
-                RACC[...] += (
-                    table[:, 0:128] + table[:, 128:256] + table[:, 256:384] + table[:, 384:512]
-                )
+                    raised = jnp.exp(mm(view, PR[:, columns]) / SHARPNESS)
+                for q in range(chunk // LANES):
+                    tile = pl.ds(pl.multiple_of(c * chunk + q * LANES, LANES), images)
+                    if first:
+                        table = raised[:, lanes(q)]
+                    else:
+                        table = TAB[tile, :] * RINV[...]
+                    total = jnp.sum(table, axis=0, keepdims=True)
+                    table = table * jnp.where(valid[:, lanes(q)], 1.0 / total, 0.0)
+                    TAB[tile, :] = table
+                    RACC[...] += table
 
             RINV[...] = jnp.broadcast_to(
                 1.0 / jnp.sum(RACC[...], axis=1, keepdims=True), (images, LANES)
@@ -769,9 +985,10 @@
 
         for number in range(SINK):
             sweep(number == 0)
-        own = pl.ds(pl.multiple_of(d * IMAGES, IMAGES), IMAGES)
-        row_inv = RINV[own, :][:, 0:1]
-        Q[pl.ds(pl.multiple_of(v * IMAGES, IMAGES), IMAGES), :] = TAB[own, :] * row_inv
+        row_inv = RINV[pl.ds(pl.multiple_of(d * IMAGES, IMAGES), IMAGES), :]
+        for c in range(PADDED // LANES):
+            own = pl.ds(pl.multiple_of(c * LANES + d * IMAGES, IMAGES), IMAGES)
+            Q[pl.ds(pl.multiple_of(v * IMAGES, IMAGES), IMAGES), lanes(c)] = TAB[own, :] * row_inv
 
     ident_f = jnp.sum(eye * crop_ids.astype(F32), axis=1, keepdims=True)
     pick_lane = lax.broadcasted_iota(jnp.int32, (SLOTS, 2 * IMAGES), 1)
@@ -783,13 +1000,12 @@
     picked = jnp.where(big, crossed.astype(F32), matched.astype(F32))
     image_weight = 1.0 / (2.0 * (1.0 + count_row[...].astype(F32)))
     picked = picked * jnp.concatenate([image_weight, image_weight], axis=1)
-    TG[...] = jnp.dot(picked, Q[...], precision=HIGH, preferred_element_type=F32)
     valid_all = lax.broadcasted_iota(jnp.int32, (1, PADDED), 1) < PROTOS
     loss_rows = []
     for s in range(4):
         rows = slice(16 * s, 16 * s + 16)
-        target = TG[rows, :]
-        logit = jnp.where(valid_all, SC[rows, :] / SOFTMAX_HEAT, -1e30)
+        target = jnp.dot(picked[rows], Q[...], precision=HIGH, preferred_element_type=F32)
+        logit = jnp.where(valid_all, mm(UL[rows, :], PR[...]) / SOFTMAX_HEAT, -1e30)
         shifted = logit - jnp.max(logit, axis=1, keepdims=True)
         raised = jnp.exp(shifted)
         total = jnp.sum(raised, axis=1, keepdims=True)
@@ -800,11 +1016,12 @@
         loss_rows[0] + loss_rows[1] + loss_rows[2] + loss_rows[3], axis=0, keepdims=True
     )
 
-    OUTP = t_mm(unit_low, DS[...])
-    PROTO_BUF = TAB
-    PROTO_BUF[...] = OUTP
-    proto_copy = pltpu.make_async_copy(PROTO_BUF, proto_out, out_sem.at[2])
-    proto_copy.start()
+    def proto_half(which):
+        return t_mm(DS[:, pl.ds(pl.multiple_of(which * PROTO_HALF, LANES), PROTO_HALF)], UL[...])
+
+    OUT_P[...] = proto_half(1 - r)
+    proto_swap = core_copy(OUT_P, RC_P, 4, 17)
+    proto_swap.start()
     unit_grad = mm_t(DS[...], PR[...])
     along = jnp.sum(unit * unit_grad, axis=1, keepdims=True)
     head_two_grad = (unit_grad - unit * along) * length_inv
@@ -826,17 +1043,29 @@
             MSG[X_FOUR_BACK + j, 4 + q : 5 + q, :] = jnp.sum(du * centred, axis=0, keepdims=True)
         announce(X_FOUR_BACK + j)
 
-    project_buf = OUTT.at[0]
-    for j in range(4):
-        project_buf[:, lanes(j)] = t_mm(A4[:, lanes(j, WIDTH)], head_two_low)
-    project_copies = [
-        pltpu.make_async_copy(
-            project_buf.at[:, lanes(j)], project_out.at[pl.ds(j * WIDTH, WIDTH), :], out_sem.at[0]
-        )
-        for j in range(4)
-    ]
-    for copy in project_copies:
-        copy.start()
+    D2F[...] = head_two_low.astype(F32)
+
+    def share_rows(depth):
+        own = pl.ds(pl.multiple_of(d * depth, 16), depth)
+
+        @pl.loop(1, GROUP)
+        def _(k):
+            pltpu.make_async_remote_copy(
+                D2F.at[pl.ds(0, depth), :],
+                D2A.at[own, :],
+                row_sem.at[1],
+                row_sem.at[2],
+                device_id=(r, lax.rem(d + k, GROUP)),
+                device_id_type=MESH,
+            ).start()
+
+        D2A[own, :] = D2F[0:depth, :]
+
+    by_size(share_rows)
+    proto_own = proto_half(r)
+    proto_swap.wait_recv()
+    RC_P[...] += proto_own
+    proto_strip.start(0)
 
     @pl.loop(0, 4)
     def _(j):
@@ -848,15 +1077,30 @@
                 DA4[j, :, lanes(q)], centred, CW[...], PRM4, 4 * j + q
             ).astype(BF)
 
+    pooled_arrived(2)
+    pooled_gather(3)
+    DP = H1
+    for j in range(4):
+        DP[j] = jnp.zeros((SLOTS, WIDTH), F32)
+
     @pl.loop(0, 4)
-    def _(j):
-        DP[j] = mm_t(DH1[...], WH[at(j * WIDTH, WIDTH), :]) * area_inv
+    def _(i):
+        for half in range(2):
+            k = 2 * i + half
+            hidden_load(k, half).wait()
+            back = mm_t(DH1[:, lanes(k, 256)], WHB[half])
+            for j in range(4):
+                DP[j] += back[:, lanes(j, WIDTH)]
+
+            @pl.when(k + 2 < 8)
+            def _():
+                hidden_load(k + 2, half).start()
 
     @pl.loop(0, 4)
     def _(j):
         rows = at(j * ROWS, ROWS)
         for q in range(4):
-            high, low = two_parts(DP[j, :, lanes(q)])
+            high, low = two_parts(DP[j, :, lanes(q)] * area_inv)
             out_grad = mm(PT[...], high) + mm(PT[...], low)
             centred, before = norm_terms(C3[rows, lanes(q)], PRM3, 4 * j + q)
             joined = before + F[:, lanes(4 * j + q)].astype(F32)
@@ -866,28 +1110,7 @@
             MSG[X_THREE_BACK + j, 4 + q : 5 + q, :] = jnp.sum(du * centred, axis=0, keepdims=True)
         announce(X_THREE_BACK + j)
 
-    pltpu.make_async_copy(project_buf, project_buf, out_sem.at[0]).wait()
-
-    def send_tile(slot, target, first):
-        copy = pltpu.make_async_copy(OUTT.at[slot], target, out_sem.at[slot])
-        if not isinstance(first, bool):
-
-            @pl.when(jnp.logical_not(first))
-            def _():
-                copy.wait()
-        elif not first:
-            copy.wait()
-        return copy
-
-    @pl.loop(0, 16)
-    def _(tile):
-        slot = lax.rem(tile, 2)
-        i = tile // 4
-        j = lax.rem(tile, 4)
-        target = hidden_out.at[at(i * WIDTH, WIDTH), lanes(j, WIDTH)]
-        copy = send_tile(slot, target, tile < 2)
-        OUTT[slot] = t_mm(PO[:, lanes(i, WIDTH)], DH1[:, lanes(j, WIDTH)])
-        copy.start()
+    advance([(proto_strip, 0)])
 
     @pl.loop(0, 4)
     def _(j):
@@ -900,32 +1123,43 @@
                 DJ[rows, lanes(q)], centred, RW[...], PRM3, 4 * j + q
             ).astype(BF)
 
+    pl.semaphore_signal(free_sem, inc=1, device_id=(1 - r, d), device_id_type=MESH)
+    centre = pl.ds(EDGE, ROWS)
+
     @pl.loop(0, 2)
     def _(h):
-        DA[:, lanes(h, 256)] = mm_t(COLS[:, 0:DEPTH], WE[at(h * 256, 256), :])
-
-    for q in range(4):
-        centred, before = norm_terms(C2[:, lanes(q)], PRM2, q)
-        du = DA[:, lanes(q)] * gelu_slope(before) * RW[...]
-        DA[:, lanes(q)] = du
-        MSG[X_TWO_BACK, q : q + 1, :] = jnp.sum(du, axis=0, keepdims=True)
-        MSG[X_TWO_BACK, 4 + q : 5 + q, :] = jnp.sum(du * centred, axis=0, keepdims=True)
-    announce(X_TWO_BACK)
+        APAD[centre, lanes(h, 256)] = mm_t(COLS[:, 0:DEPTH], WE[at(h * 256, 256), :])
+
+    def through_gelu(values, prm, x):
+        for q in range(4):
+            centred, before = norm_terms(values[:, lanes(q)], prm, q)
+            du = APAD[centre, lanes(q)] * gelu_slope(before) * RW[...]
+            APAD[centre, lanes(q)] = du
+            MSG[x, q : q + 1, :] = jnp.sum(du, axis=0, keepdims=True)
+            MSG[x, 4 + q : 5 + q, :] = jnp.sum(du * centred, axis=0, keepdims=True)
+        announce(x)
+
+    through_gelu(C2, PRM2, X_TWO_BACK)
 
     @pl.loop(0, 4)
     def _(j):
-        slot = lax.rem(j, 2)
-        copy = send_tile(slot, expand_out.at[:, lanes(j, WIDTH)], False)
-        OUTT[slot] = t_mm(A2[...], COLS[:, lanes(j, WIDTH)])
-        copy.start()
-
+        OUT[half_tile(j), :] = t_mm(A2[:, half_tile(1 - r)], COLS[:, lanes(j, WIDTH)])
+        core_copy(OUT.at[half_tile(j), :], RC_E.at[half_tile(j), :], j, j).start()
+
+    @pl.loop(0, 4)
+    def _(j):
+        own = t_mm(A2[:, half_tile(r)], COLS[:, lanes(j, WIDTH)])
+        tile = RC_E.at[half_tile(j), :]
+        core_copy(tile, tile, j, j).wait_recv()
+        tile[...] += own
+
+    for strip in expand_strips:
+        strip.start(0)
     collect(X_TWO_BACK)
     whole_back(X_TWO_BACK, whole_rows, PRM2, 0, 4)
     for q in range(4):
         centred, _ = norm_terms(C2[:, lanes(q)], PRM2, q)
-        APAD[EDGE : EDGE + ROWS, lanes(q)] = back_through(
-            DA[:, lanes(q)], centred, RW[...], PRM2, q
-        )
+        APAD[centre, lanes(q)] = back_through(APAD[centre, lanes(q)], centred, RW[...], PRM2, q)
     spread_taps(-1)
 
     @pl.loop(0, 2)
@@ -935,25 +1169,75 @@
             total += mm_t(
                 COLS[:, tap * WIDTH : (tap + 1) * WIDTH], WS[at(tap * WIDTH + h * 256, 256), :]
             )
-        DA[:, lanes(h, 256)] = total
-
-    for q in range(4):
-        centred, before = norm_terms(C1[:, lanes(q)], PRM1, q)
-        du = DA[:, lanes(q)] * gelu_slope(before) * RW[...]
-        DA[:, lanes(q)] = du
-        MSG[X_ONE_BACK, q : q + 1, :] = jnp.sum(du, axis=0, keepdims=True)
-        MSG[X_ONE_BACK, 4 + q : 5 + q, :] = jnp.sum(du * centred, axis=0, keepdims=True)
-    announce(X_ONE_BACK)
+        APAD[centre, lanes(h, 256)] = total
+
+    through_gelu(C1, PRM1, X_ONE_BACK)
+    advance([(proto_strip, 1)])
+
+    def half_tap(which, m):
+        g = 9 * which + m
+        return mm(A1T[half_tile(lax.rem(g, 2)), :], COLS[:, lanes(g // 2, WIDTH)])
+
+    pl.semaphore_wait(free_sem, 1)
+
+    def ring(slot):
+        tile = OUT.at[half_tile(slot), :]
+        return tile, core_copy(tile, tile, slot, 0)
+
+    def add_half_tap(m):
+        own = half_tap(r, m)
+        tile = C3.at[half_tile(m), :]
+        core_copy(tile, tile, 0, 4 + m).wait_recv()
+        tile[...] += own
 
     @pl.loop(0, 9)
-    def _(tap):
-        slot = lax.rem(tap, 2)
-        copy = send_tile(slot, spatial_out.at[at(tap * WIDTH, WIDTH), :], False)
-        OUTT[slot] = mm(A1T[...], COLS[:, lanes(tap, WIDTH)])
-        copy.start()
+    def _(m):
+        slot = lax.rem(m, 4)
+        tile, last = ring(slot)
+        last.wait_send()
+        tile[...] = half_tap(1 - r, m)
+        core_copy(tile, C3.at[half_tile(m), :], slot, 4 + m).start()
+
+        @pl.when(m >= 2)
+        def _():
+            add_half_tap(m - 2)
+
+    add_half_tap(7)
+    add_half_tap(8)
+    for strip in spatial_strips:
+        strip.start(0)
 
     collect(X_ONE_BACK)
     whole_back(X_ONE_BACK, whole_rows, PRM1, 0, 0)
+    for q in range(4):
+        centred, _ = norm_terms(C1[:, lanes(q)], PRM1, q)
+        A2[:, lanes(q)] = back_through(APAD[centre, lanes(q)], centred, RW[...], PRM1, q).astype(BF)
+
+    def reduce_tile(which, j):
+        columns = pl.ds(pl.multiple_of(which * 1024 + j * 256, 256), 256)
+        return t_mm(F[:, columns], A2[...])
+
+    def reduce_rows(j):
+        return C3.at[pl.ds(pl.multiple_of(SPATIAL_HALF + j * 256, 256), 256), :]
+
+    @pl.loop(0, 4)
+    def _(j):
+        slot = lax.rem(j + 1, 4)
+        tile, last = ring(slot)
+        last.wait_send()
+        tile[...] = reduce_tile(1 - r, j)
+        core_copy(tile, reduce_rows(j), slot, 13 + j).start()
+
+    @pl.loop(0, 4)
+    def _(j):
+        own = reduce_tile(r, j)
+        tile = reduce_rows(j)
+        core_copy(tile, tile, 0, 13 + j).wait_recv()
+        tile[...] += own
+
+    for strip in reduce_strips:
+        strip.start(0)
+
     collect(X_EXTRA)
     extra = jnp.sum(RECV[X_EXTRA], axis=0)
     FAR[0, 88:96, :] = extra
@@ -966,9 +1250,11 @@
         device_id_type=MESH,
     )
     far.start()
-    for q in range(4):
-        centred, _ = norm_terms(C1[:, lanes(q)], PRM1, q)
-        A2[:, lanes(q)] = back_through(DA[:, lanes(q)], centred, RW[...], PRM1, q).astype(BF)
+
+    def wave(strips, stage):
+        return [(strip, stage) for strip in strips]
+
+    advance(wave(expand_strips, 0))
 
     @pl.loop(0, 4)
     def _(j):
@@ -977,33 +1263,192 @@
         for q in range(4):
             DJ[rows, lanes(q)] = (DJ[rows, lanes(q)] + grad[:, lanes(q)]) * RW[...]
         pltpu.make_async_copy(
-            DJ.at[rows, :], feature_out.at[0, :, lanes(j, WIDTH)], out_sem.at[3]
+            DJ.at[rows, :], feature_out.at[0, :, lanes(j, WIDTH)], out_sem.at[0]
         ).start()
 
-    @pl.loop(0, 4)
-    def _(j):
-        slot = lax.rem(j + 1, 2)
-        copy = send_tile(slot, reduce_out.at[at(j * WIDTH, WIDTH), :], False)
-        OUTT[slot] = t_mm(F[:, lanes(j, WIDTH)], A2[...])
-        copy.start()
-
+    advance(wave(expand_strips, 1))
+    advance(wave(spatial_strips, 0))
+
+    pooled_arrived(3)
+
+    def rows_in(depth):
+        area = D2A.at[pl.ds(0, (GROUP - 1) * depth), :]
+        pltpu.make_async_copy(area, area, row_sem.at[2]).wait()
+        pltpu.make_async_copy(area, area, row_sem.at[1]).wait()
+
+    by_size(rows_in)
+    loads[4].wait()
+    for slot in range(4):
+        ring(slot)[1].wait_send()
+    CH = OUT
+    HACC[...] = jnp.zeros_like(HACC)
+    PACC[...] = jnp.zeros_like(PACC)
+    unit_rows = pl.ds(pl.multiple_of(d * LANES, LANES), LANES)
+
+    @pl.loop(0, jnp.where(big, 1, 4))
+    def _(c):
+        rows = half_tile(c)
+        for j in range(4):
+            pltpu.make_async_copy(
+                PG.at[rows, lanes(j, WIDTH)], CH.at[pl.ds(256 * j, 256), :], out_sem.at[1]
+            ).start()
+        pltpu.make_async_copy(CH, CH, out_sem.at[1]).wait()
+        head = mm(CH[0:256, :].astype(BF), WHC[0:WIDTH, :])
+        for j in range(1, 4):
+            head += mm(CH[256 * j : 256 * j + 256, :].astype(BF), WHC[WIDTH * j : WIDTH * j + WIDTH, :])
+        centred, before = norm_terms(head, PRM4, d)
+        low_rows = D2A[rows, :].astype(BF)
+        du = mm_t(low_rows, WP[unit_rows, :]) * gelu_slope(before)
+        dh = back_through(du, centred, 1.0, PRM4, d).astype(BF)
+        PACC[...] += t_mm(gelu(before).astype(BF), low_rows)
+        for j in range(4):
+            HACC[WIDTH * j : WIDTH * j + WIDTH, :] += t_mm(
+                CH[256 * j : 256 * j + 256, :].astype(BF), dh
+            )
+
+    def hidden_half(which):
+        return HACC.at[pl.ds(pl.multiple_of(which * 1024, 1024), 1024), :]
+
+    hidden_swap = core_copy(hidden_half(1 - r), HREC, 5, 18)
+    hidden_swap.start()
+    project_swap = core_copy(PACC, PREC, 6, 19)
+    project_swap.start()
+    advance([(proto_strip, 2)])
+    hidden_swap.wait_recv()
+    hidden_half(r)[...] += HREC[...]
+
+    @pl.loop(1, GROUP)
+    def _(k):
+        to = lax.rem(d + k, GROUP)
+        pltpu.make_async_remote_copy(
+            HACC.at[pl.ds(pl.multiple_of(r * 1024 + to * 64, 64), 64), :],
+            HAL.at[d],
+            row_sem.at[3],
+            row_sem.at[4],
+            device_id=(r, to),
+            device_id_type=MESH,
+        ).start()
+
+    HAL[d] = HACC[pl.ds(pl.multiple_of(r * 1024 + d * 64, 64), 64), :]
+
+    project_swap.wait()
+    PACC[...] = jnp.where(big, PACC[...], PREC[...]) + jnp.where(big, PREC[...], PACC[...])
+    serves = (d // 8) == r
+    first_owner = lax.rem(2 * d, GROUP)
+    for half in range(2):
+        owner = first_owner + half
+        part = PACC.at[pl.ds(64 * half, 64), :]
+        local = owner == d
+
+        @pl.when(serves & jnp.logical_not(local))
+        def _():
+            pltpu.make_async_remote_copy(
+                part, PIN, core_send.at[7 + half], row_sem.at[5],
+                device_id=(r, owner), device_id_type=MESH,
+            ).start()
+
+        @pl.when(serves & local)
+        def _():
+            PIN[...] = part[...]
+
+    chip_of_own = (r * GROUP + d) // 2
+    from_self = chip_of_own == d
+
+    advance(wave(reduce_strips, 0))
+    advance(wave(expand_strips, 2))
+    advance(wave(spatial_strips, 1))
+    advance([(proto_strip, 3)])
+    proto_own_rows = pl.ds(pl.multiple_of(r * PROTO_HALF + d * 96, 16), 96)
+    TAB[proto_own_rows, :] = RC_P[pl.ds(pl.multiple_of(d * 96, 16), 96), :]
+    proto_order = (8, 2, 1, 4)
+    every_lane = slice(0, LANES)
+
+    def proto_gather(stage):
+        gather_start(TAB, r * PROTO_HALF, 96, every_lane, proto_order, stage, 3)
+
+    def proto_arrived(stage):
+        gather_wait(TAB, 96, every_lane, stage, 3, gather_recv)
+
+    proto_gather(0)
+    advance(wave(reduce_strips, 1))
+    proto_arrived(0)
+    proto_gather(1)
+    advance(wave(expand_strips, 3))
+    advance(wave(spatial_strips, 2))
+    proto_arrived(1)
+    proto_gather(2)
+    advance(wave(reduce_strips, 2))
+    proto_arrived(2)
+    proto_gather(3)
+    for j in range(4):
+        for q in range(4):
+            expand_out[pl.ds(4 * j + q, 16, stride=16), :] = RC_E[
+                pl.ds(pl.multiple_of(256 * j + d * 16, 16), 16), lanes(q)
+            ]
     far.wait()
     both = jnp.where(big, FAR[0], FAR[1]) + jnp.where(big, FAR[1], FAR[0])
     gain_out[...] = both[0:40]
     shift_out[0:40, :] = both[48:88]
     shift_out[40:41, :] = both[88:89]
     loss_out[...] = jnp.broadcast_to(both[89:90], (8, LANES)) / float(GROUP * IMAGES)
+    arrived = HAL.at[pl.ds(0, GROUP - 1)]
+    pltpu.make_async_copy(arrived, arrived, row_sem.at[4]).wait()
+    pltpu.make_async_copy(arrived, arrived, row_sem.at[3]).wait()
+    for source in range(GROUP):
+        hidden_out[pl.ds(source, 64, stride=16), :] = HAL[source]
+
+    @pl.when(jnp.logical_not(from_self))
+    def _():
+        pltpu.make_async_copy(PIN, PIN, row_sem.at[5]).wait()
+
+    project_out[...] = PIN[...]
+    for half in range(2):
+
+        @pl.when(serves & jnp.logical_not(first_owner + half == d))
+        def _():
+            pltpu.make_async_copy(PIN, PIN, core_send.at[7 + half]).wait()
+
+    proto_arrived(3)
+    proto_part = TAB.at[pl.ds(pl.multiple_of(r * PROTO_HALF, LANES), PROTO_HALF), :]
+    proto_far = core_copy(proto_part, proto_part, 9, 20)
+    proto_far.start()
+    advance(wave(spatial_strips, 3))
+    for q in range(4):
+        spatial_out[pl.ds(q, 144, stride=4), :] = C3[
+            pl.ds(pl.multiple_of(d * 144, 16), 144), lanes(q)
+        ]
+    proto_far.wait()
+    for m in range(6):
+        for q in range(4):
+            chunk_rows = pl.ds((4 * m + q) * LANES, LANES)
+            CH[LANES * m : LANES * m + LANES, lanes(q)] = TAB[chunk_rows, :].T
+        pltpu.make_async_copy(
+            CH.at[pl.ds(LANES * m, LANES), :], proto_out.at[:, lanes(m, WIDTH)], out_sem.at[2]
+        ).start()
+    advance(wave(reduce_strips, 3))
+    for q in range(4):
+        reduce_out[pl.ds(q, 64, stride=4), :] = C3[
+            pl.ds(pl.multiple_of(SPATIAL_HALF + d * 64, 16), 64), lanes(q)
+        ]
 
     @pl.when(big)
     def _():
         forward_units.wait_send()
 
-    proto_copy.wait()
-    for slot in range(2):
-        pltpu.make_async_copy(
-            OUTT.at[slot], reduce_out.at[pl.ds(0, WIDTH), :], out_sem.at[slot]
-        ).wait()
-    pltpu.make_async_copy(feature_out.at[0], feature_out.at[0], out_sem.at[3]).wait()
+    hidden_swap.wait_send()
+    proto_swap.wait_send()
+    for stage in range(4):
+
+        def pooled_sent(depth):
+            for number, (columns, _) in enumerate(pooled_parts):
+                gather_wait(PG, depth, columns, stage, number, gather_send)
+
+        by_size(pooled_sent)
+        gather_wait(TAB, 96, every_lane, stage, 3, gather_send)
+    for strip in spatial_strips + reduce_strips + expand_strips + [proto_strip]:
+        strip.close()
+    pltpu.make_async_copy(feature_out.at[0], feature_out.at[0], out_sem.at[0]).wait()
+    pltpu.make_async_copy(proto_out, proto_out, out_sem.at[2]).wait()
 
 
 def tower(
@@ -1022,6 +1467,7 @@
     protos = jnp.pad(prototypes, ((0, 0), (0, PADDED - PROTOS)))
     anywhere = pl.BlockSpec(memory_space=pl.ANY)
     inside = pl.BlockSpec(memory_space=pltpu.VMEM)
+    in_hbm = pl.BlockSpec(memory_space=pltpu.HBM)
 
     def vm(*shape, dtype=F32):
         return pltpu.VMEM(shape, dtype)
@@ -1036,30 +1482,37 @@
         out_shape=(
             shaped(8, LANES),
             shaped(1, ROWS, DEPTH),
-            shaped(DEPTH, WIDTH),
-            shaped(9 * WIDTH, WIDTH),
-            shaped(WIDTH, DEPTH),
-            shaped(DEPTH, HIDDEN),
-            shaped(HIDDEN, FEATS),
+            shaped(256, LANES),
+            shaped(576, LANES),
+            shaped(256, LANES),
+            shaped(1024, LANES),
+            shaped(64, LANES),
             shaped(FEATS, PADDED),
             shaped(40, LANES),
             shaped(41, LANES),
+            shaped(GROUP * SLOTS, DEPTH),
+            shaped(4, 15 * 144, LANES),
+            shaped(4, 15 * 64, LANES),
+            shaped(4, 15 * 16, WIDTH),
+            shaped(15 * 96, LANES),
         ),
         in_specs=[anywhere, inside, inside] + [anywhere] * 6 + [inside, inside],
-        out_specs=(inside,) + (anywhere,) * 7 + (inside, inside),
+        out_specs=(
+            (inside, anywhere) + (inside,) * 5 + (anywhere, inside, inside) + (in_hbm,) * 5
+        ),
         scratch_shapes=[
             vm(ROWS, DEPTH, dtype=BF),
             vm(DEPTH, WIDTH, dtype=BF),
             vm(9 * WIDTH, WIDTH, dtype=BF),
             vm(WIDTH, DEPTH, dtype=BF),
-            vm(DEPTH, HIDDEN, dtype=BF),
+            vm(2, DEPTH, 256, dtype=BF),
+            vm(DEPTH, LANES, dtype=BF),
             vm(HIDDEN, FEATS, dtype=BF),
             vm(FEATS, PADDED, dtype=BF),
             vm(ROWS, WIDTH),
             vm(ROWS, WIDTH),
+            vm(SPATIAL_HALF + 1024, WIDTH),
             vm(4 * ROWS, WIDTH),
-            vm(4 * ROWS, WIDTH),
-            vm(ROWS, WIDTH),
             vm(ROWS + 2 * EDGE, WIDTH),
             vm(ROWS, 9 * WIDTH, dtype=BF),
             vm(ROWS, WIDTH, dtype=BF),
@@ -1069,11 +1522,12 @@
             vm(SLOTS, HIDDEN, dtype=BF),
             vm(4, SLOTS, WIDTH),
             vm(SLOTS, HIDDEN, dtype=BF),
-            vm(4, SLOTS, WIDTH),
-            vm(SLOTS, PADDED),
-            vm(SLOTS, PADDED),
             vm(SLOTS, PADDED, dtype=BF),
-            vm(GROUP * IMAGES, PADDED),
+            vm(SLOTS, FEATS, dtype=BF),
+            vm(SLOTS, DEPTH),
+            vm(SLOTS, FEATS),
+            vm(GROUP * SLOTS, FEATS),
+            vm(PADDED, GROUP * IMAGES),
             vm(2 * IMAGES, PADDED),
             vm(GROUP * IMAGES, LANES),
             vm(GROUP * IMAGES, LANES),
@@ -1091,17 +1545,38 @@
             vm(16, 8, LANES),
             vm(EXCHANGES, 8, LANES),
             vm(EXCHANGES, GROUP, 8, LANES),
-            vm(2, WIDTH, WIDTH),
+            vm(2, 96, LANES),
+            vm(1024, WIDTH),
+            vm(1024, WIDTH),
+            vm(PROTO_HALF, LANES),
+            vm(PROTO_HALF, LANES),
+            vm(2, 8 * 144, LANES),
+            vm(2, 8 * 16, WIDTH),
+            vm(DEPTH, LANES),
+            vm(1024, LANES),
+            vm(GROUP, 64, LANES),
+            vm(LANES, LANES),
+            vm(LANES, LANES),
+            vm(64, LANES),
             dma((7,)),
             dma((EXCHANGES,)),
             dma((EXCHANGES,)),
             dma((4,)),
             dma((4,)),
             dma((2,)),
-            vm(2, 96, LANES),
+            dma((2,)),
+            dma((13, 4)),
+            dma((13, 4)),
+            dma((2,)),
+            dma((4, 4)),
+            dma((4, 4)),
+            dma((10,)),
+            dma((21,)),
+            dma((6,)),
+            pltpu.SemaphoreType.REGULAR,
         ],
         compiler_params=pltpu.CompilerParams(
-            collective_id=0, has_side_effects=True, vmem_limit_bytes=62 << 20
+            collective_id=0, has_side_effects=True, vmem_limit_bytes=63 << 20
         ),
     )(
         features,
@@ -1119,22 +1594,16 @@
 
 
 def fused_body(*arrays):
-    loss, feature_grad, reduce, spatial, expand, hidden, project, proto, gain, shift = tower(*arrays)
-
-    def scattered(grad):
-        return lax.psum_scatter(
-            grad.reshape(-1), ("res", "dp"), scatter_dimension=0, tiled=True
-        )
-
+    loss, feature, reduce, spatial, expand, hidden, project, proto, gain, shift = tower(*arrays)[:10]
     return (
         loss[0, 0],
-        feature_grad,
-        scattered(reduce),
-        scattered(spatial),
-        scattered(expand),
-        scattered(hidden),
-        scattered(project),
-        lax.psum(proto[:, :PROTOS].reshape(-1), ("res", "dp")),
+        feature,
+        reduce.reshape(-1),
+        spatial.reshape(-1),
+        expand.reshape(-1),
+        hidden.reshape(-1),
+        project.reshape(-1),
+        proto[:, :PROTOS].reshape(-1),
         gain.reshape(-1),
         shift.reshape(-1),
     )

time: 747 us -> 292 us (0.39)
  waiting for transfers between devices: 549 us -> 0 us
  Pallas kernels: 127 us -> 271 us
  local copies, waits for them, and re-layouts: 57 us -> 18.4 us
  between operations: 14.1 us -> 0.69 us
    unnamed x2 -> x0, waiting for transfers between devices: 549 us -> none
    pallas_call x1, Pallas kernels: 127 us -> 271 us  [tower(): pl.pallas_call(tower_kernel, out_shape=(shaped(8, LANES), shaped(1, ROWS,...]
    unnamed x22 -> x23, local copies, waits for them, and re-layouts: 52.7 us -> 12.6 us
  transfers between devices with their start and end apart: 1 -> 0, of which waited for: 1 -> 0; matrix products, arithmetic and copies ran while one was open for 0% -> 0% of each run, Pallas kernels for 0% -> 0%
where the time goes in v2:
time: 292 us; the launch traced here: 290 us
  Pallas kernels  271 us (93%)
  local copies, waits for them, and re-layouts  18.4 us (6%)
    pallas_call x1, Pallas kernels, tower(): pl.pallas_call(tower_kernel, out_shape=(shaped(8, LANES), shaped(1, ROWS,...  271 us
    unnamed x23, local copies, waits for them, and re-layouts  12.6 us

profile of v2, /device:TPU:0, one launch (start us, length us, event | category | flops | bytes accessed | tf_op | source)
XLA Modules:
  0.0 290.2 jit_solution(14992590333734904160)
XLA Ops:
  0.6 1.4 copy.22
  2.1 0.9 pad.4.protos
  3.0 271.2 %shard_map.186 = (f32[8,128]{1,0:T(8,128)}, f32[1,784,2048]{2,1,0:T(8,128)}, f32[256,128]{1,0:T(8,128)}, f32[576,128]{1,0:T(8,128)}, f32[256,128]{1,0:T(8,128)},...) custom-call(bf16[1,784,2048]{2,1,0:T(8,128)(2,1)} %feat.1, ...), custom_call_target="tpu_custom_call" | custom-call | tf_op jit(solution)/shard_map/pallas_call | solution.py:1480
  274.2 1.2 slice.6
  275.4 3.6 %reshape.65 = f32[384000]{0:T(1024)} reshape(f32[128,3000]{1,0:T(8,128)} %bitcast.13) | data formatting | bytes 3072000 | tf_op jit(solution)/shard_map/reshape | solution.py:1606
  279.0 0.0 copy-start.3
  279.0 0.0 copy-start.1
  279.0 0.0 copy-start.2
  279.0 0.0 copy-start
  279.0 0.0 copy-start.4
  279.0 0.0 copy-start.6
  279.0 0.0 copy-start.5
  279.0 6.5 %copy.31 = f32[1,784,2048]{2,1,0:T(8,128)} copy(f32[1,784,2048]{2,1,0:T(8,128)} %get-tuple-element.41) | data formatting | bytes 12845056
  285.5 0.0 copy-done.3
  285.5 0.7 copy.32
  286.2 0.0 copy-done.1
  286.2 0.7 copy.33
  286.9 0.0 copy-done.2
  286.9 0.7 copy.34
  287.6 0.0 copy-done
  287.6 0.8 copy.35
  288.4 0.0 copy-done.4
  288.4 0.6 copy.36
  289.0 0.0 copy-done.6
  289.0 0.6 copy.37
  289.6 0.0 copy-done.5
  289.6 0.6 copy.38
Async XLA Ops:
  279.0 6.5 %copy-start.3 = (f32[256,128]{1,0:T(8,128)S(1)}, f32[256,128]{1,0:T(8,128)}, u32[]{:S(2)}) copy-start(f32[256,128]{1,0:T(8,128)} %get-tuple-element.22) | copy-start | bytes 393220
  279.0 7.2 %copy-start.1 = (f32[576,128]{1,0:T(8,128)S(1)}, f32[576,128]{1,0:T(8,128)}, u32[]{:S(2)}) copy-start(f32[576,128]{1,0:T(8,128)} %get-tuple-element.23) | copy-start | bytes 884740
  279.0 7.9 %copy-start.2 = (f32[256,128]{1,0:T(8,128)S(1)}, f32[256,128]{1,0:T(8,128)}, u32[]{:S(2)}) copy-start(f32[256,128]{1,0:T(8,128)} %get-tuple-element.24) | copy-start | bytes 393220
  279.0 8.6 %copy-start = (f32[1024,128]{1,0:T(8,128)S(1)}, f32[1024,128]{1,0:T(8,128)}, u32[]{:S(2)}) copy-start(f32[1024,128]{1,0:T(8,128)} %get-tuple-element.25) | copy-start | bytes 1572868
  279.0 9.4 %copy-start.4 = (f32[64,128]{1,0:T(8,128)S(1)}, f32[64,128]{1,0:T(8,128)}, u32[]{:S(2)}) copy-start(f32[64,128]{1,0:T(8,128)} %get-tuple-element.26) | copy-start | bytes 98308
  279.0 10.0 %copy-start.6 = (f32[40,128]{1,0:T(8,128)S(1)}, f32[40,128]{1,0:T(8,128)}, u32[]{:S(2)}) copy-start(f32[40,128]{1,0:T(8,128)} %get-tuple-element.28) | copy-start | bytes 61444
  279.0 10.6 %copy-start.5 = (f32[41,128]{1,0:T(8,128)S(1)}, f32[41,128]{1,0:T(8,128)}, u32[]{:S(2)}) copy-start(f32[41,128]{1,0:T(8,128)} %get-tuple-element.29) | copy-start | bytes 62980
